TPU v7x, 512 devices: a whole 4x4x16 slice. The times are simulated.
512 devices in a mesh: wide: 32 (over x, y, z_hi), narrow: 16 (over z_lo, core).
Axes of the slice: x: 4, y: 4, z: 16 (z_hi: 2, z_lo: 8; z = z_hi * 8 + z_lo), core: 2. Of those that a mesh axis runs over, the one named last changes fastest.
Arguments:
- x_row_codes: bfloat16 [512, 18432], P(('narrow', 'wide')), may hold values from -3.75 to 3.75, as said below
- x_row_scales: int32 [512, 576], P(('narrow', 'wide')), may hold values from -2 to 1
- x_col_codes: bfloat16 [512, 18432], P(None, ('narrow', 'wide')), may hold values from -3.75 to 3.75, as said below
- x_col_scales: int32 [16, 18432], P(None, ('narrow', 'wide')), may hold values from -2 to 1
- grad_out: bfloat16 [512, 18432], P(('narrow', 'wide')), may hold values from -6 to 6
- up_weight: bfloat16 [18432, 8192], P('narrow', 'wide'), may hold values from -0.046875 to 0.046875
- down_weight: bfloat16 [8192, 18432], P('wide', 'narrow'), may hold values from -0.0625 to 0.0625
Outputs:
- input_grad: bfloat16 [512, 18432], P('wide', 'narrow')
- up_grad: float32 [18432, 8192], P('narrow', 'wide')
- down_grad: float32 [8192, 18432], P('wide', 'narrow')
Inputs may be any that keep to these rules, and one draw needn't show every extreme that they name: `x_row_codes`: every entry is an E4M3 number s (1 + m/8) 2^e with s = -1 or 1, m of 0 to 7 and e of -3 to 1. `x_col_codes`: every entry is an E4M3 number s (1 + m/8) 2^e with s = -1 or 1, m of 0 to 7 and e of -3 to 1.
All inputs are finite; a program needn't handle non-finite values.
Results may differ from a plain program's by a relative error of at most 0.005.
Values may be sent and summed in bfloat16 or wider, within the bound.
No kernel may reach another device: no remote copies, remote signals or barrier semaphores. Data moves between devices by JAX's collectives and lax.ppermute only.
A program may use at most 64 MiB of HBM per device.

v0:
```python
import jax
import jax.numpy as jnp
from jax import lax
from jax.sharding import PartitionSpec as P


def dequant_rows(codes, exps):
    tok_count, col_count = codes.shape
    blocks = codes.astype(jnp.float32).reshape(tok_count, col_count // 32, 32)
    blocks = blocks * jnp.exp2(exps.astype(jnp.float32))[:, :, None]
    return blocks.reshape(tok_count, col_count).astype(jnp.bfloat16)


def dequant_cols(codes, exps):
    tok_count, col_count = codes.shape
    blocks = codes.astype(jnp.float32).reshape(tok_count // 32, 32, col_count)
    blocks = blocks * jnp.exp2(exps.astype(jnp.float32))[:, None, :]
    return blocks.reshape(tok_count, col_count).astype(jnp.bfloat16)


def nonlinear(pre, act_grad):
    positive = jnp.maximum(pre, 0.0)
    squared = (positive * positive).astype(jnp.bfloat16)
    hidden_grad = (act_grad * 2.0 * positive).astype(jnp.bfloat16)
    return (squared, hidden_grad)


def body(x_row_codes, x_row_scales, x_col_codes, x_col_scales, grad_out, up_weight, down_weight):
    x_row = dequant_rows(x_row_codes, x_row_scales)
    whole_x, whole_g = (
        lax.all_gather(x_row, "wide", axis=0, tiled=True),
        lax.all_gather(grad_out, "wide", axis=0, tiled=True),
    )
    x_cols, g_cols = (
        lax.all_to_all(whole_x, "narrow", split_axis=1, concat_axis=0, tiled=True),
        lax.all_to_all(whole_g, "narrow", split_axis=1, concat_axis=0, tiled=True),
    )
    pre_part = jnp.dot(x_cols, up_weight, preferred_element_type=jnp.float32)
    grad_part = jnp.einsum("td,fd->tf", g_cols, down_weight, preferred_element_type=jnp.float32)
    pre, act_grad = lax.psum((pre_part, grad_part), "narrow")
    squared, hidden_grad = nonlinear(pre, act_grad)
    down_grad = jnp.einsum("tf,td->fd", squared, g_cols, preferred_element_type=jnp.float32)
    x_col = dequant_cols(x_col_codes, x_col_scales)
    up_grad = jnp.einsum(
        "tk,tf->kf",
        lax.all_gather(x_col, "wide", axis=1, tiled=True),
        hidden_grad,
        preferred_element_type=jnp.float32,
    )
    input_grad = lax.psum_scatter(
        jnp.einsum("tf,df->td", hidden_grad, up_weight, preferred_element_type=jnp.float32),
        "wide",
        scatter_dimension=0,
        tiled=True,
    ).astype(jnp.bfloat16)
    return (input_grad, up_grad, down_grad)


def solution(mesh):
    in_specs = (
        P(("narrow", "wide"), None),
        P(("narrow", "wide"), None),
        P(None, ("narrow", "wide")),
        P(None, ("narrow", "wide")),
        P(("narrow", "wide"), None),
        P("narrow", "wide"),
        P("wide", "narrow"),
    )
    out_specs = (P("wide", "narrow"), P("narrow", "wide"), P("wide", "narrow"))
    return jax.shard_map(body, mesh=mesh, in_specs=in_specs, out_specs=out_specs, check_vma=False)
```

profile of v0, /device:TPU:1, one launch (start us, length us, event | category | flops | bytes accessed | tf_op | source)
XLA Modules:
  0.0 1019.7 jit_solution(16151036481507497131)
XLA Ops:
  7.2 0.0 copy-start
  7.2 0.0 all-gather.7.cloned.1.call-start
  7.2 0.7 all-gather.7.cloned.1.call-update
  7.9 0.7 exponential_reduce_fusion
  8.6 0.1 mul.39
  8.8 0.2 mul.40
  8.9 143.3 %all-gather.7.cloned.1.call-done = bf16[32,1,18432]{2,1,0:T(2,128)(2,1)} async-done(((bf16[1,1,18432]{2,1,0:T(2,128)(2,1)}), bf16[32,1,18432]{2,1,0:T(2,128)(2,1)}) %all-gather.7.cloned.1.call-update) | async-done | bytes 1179664 | tf_op jit(solution)/shard_map/all_gather | solution.py:32
  152.2 8.2 reduce
  160.4 1.1 copy.22
  161.5 0.0 copy-start.3
  161.5 5.9 all-to-all-start
  167.4 0.2 all-gather.9.cloned.1.call-start
  167.7 0.0 copy-done.3
  167.7 0.7 convert_bitcast_fusion
  168.4 0.0 all-gather.9.cloned.1.call-update
  168.4 140.7 %all-gather.9.cloned.1.call-done = bf16[32,1,18432]{2,1,0:T(2,128)(2,1)} async-done(((bf16[1,1,18432]{2,1,0:T(2,128)(2,1)}), bf16[32,1,18432]{2,1,0:T(2,128)(2,1)}) %all-gather.9.cloned.1.call-update) | async-done | bytes 1179664 | tf_op jit(solution)/shard_map/all_gather | solution.py:31
  309.2 8.2 reduce.2
  317.4 1.1 copy.21
  318.5 0.0 all-to-all-done
  318.5 0.0 copy-start.2
  318.5 5.9 all-to-all-start.1
  324.4 0.0 all-reduce.3.cloned.1.call-start
  324.4 0.0 copy-done.2
  324.4 1.3 fusion.4
  325.8 47.7 %all-to-all-done.1 = bf16[32,16,1152]{2,0,1:T(8,128)(2,1)S(1)} async-done(((bf16[32,16,1152]{2,0,1:T(8,128)(2,1)}), bf16[32,16,1152]{2,0,1:T(8,128)(2,1)S(1)}, u32[]{:S(2)}, u32[]{:S(2)}) %all-to-all-start.1) | async-done | bytes 1179680 | tf_op jit(solution)/shard_map/all_to_all | solution.py:35
  373.4 0.0 copy-done
  373.4 0.0 copy-start.5
  373.4 1.3 fusion.5
  374.7 0.0 copy-start.4
  374.7 0.0 all-reduce.3.cloned.1.call-update
  374.8 0.0 all-gather.11.cloned.1.call-start
  374.8 0.0 copy-done.5
  374.8 0.1 copy.16
  374.9 0.1 mul.43
  375.1 0.2 mul.44
  375.2 0.3 copy-done.4
  375.5 0.6 fusion.2
  376.1 0.0 all-gather.11.cloned.1.call-update
  376.2 0.0 reduce-scatter.2.cloned.1.call-start
  376.2 196.2 %all-reduce.3.cloned.1.call-done = (f32[512,256]{1,0:T(8,128)}, f32[512,256]{1,0:T(8,128)}) async-done(((f32[512,256]{1,0:T(8,128)}, f32[512,256]{1,0:T(8,128)}), (f32[512,256]{1,0:T(8,128)}, f32[512,256]{1,0:T(8,128)})) %all-reduce.3.cloned.1.call-update) | async-done | bytes 1048592 | tf_op jit(solution)/shard_map/psum | solution.py:40
  572.4 1.3 multiply_convert_fusion.1
  573.7 2.0 fusion.6
  575.6 0.0 reduce-scatter.2.cloned.1.call-update
  575.7 117.3 %all-gather.11.cloned.1.call-done = bf16[32,36,512]{2,1,0:T(8,128)(2,1)} async-done(((bf16[1,36,512]{2,1,0:T(8,128)(2,1)}), bf16[32,36,512]{2,1,0:T(8,128)(2,1)}) %all-gather.11.cloned.1.call-update) | async-done | bytes 1179664 | tf_op jit(solution)/shard_map/all_gather | solution.py:46
  693.0 2.1 reshape.41
  695.1 0.0 copy-start.1
  695.2 1.5 fusion.7
  696.6 0.0 copy-done.1
  696.6 1.6 fusion
  698.2 313.5 %reduce-scatter.2.cloned.1.call-done = f32[16,1152]{1,0:T(8,128)} async-done(((f32[512,1152]{1,0:T(8,128)}), f32[16,1152]{1,0:T(8,128)}) %reduce-scatter.2.cloned.1.call-update) | async-done | bytes 73744 | tf_op jit(solution)/shard_map/reduce_scatter | solution.py:50
  1011.7 1.5 convert_element_type.33
  (1 shorter events, 0.0 us)
Async XLA Ops:
  7.2 366.3 %copy-start = (bf16[1152,256]{1,0:T(8,128)(2,1)S(1)}, bf16[1152,256]{1,0:T(8,128)(2,1)}, u32[]{:S(2)}) copy-start(bf16[1152,256]{1,0:T(8,128)(2,1)} %param.12) | copy-start | bytes 1769476
  7.2 145.0 %all-gather.7.cloned.1.call-start = ((), (), s32[]{:S(2)}) async-start(), calls=%async_computation.4 | async-start | bytes 2433024 | tf_op jit(solution)/shard_map/all_gather | solution.py:32
  161.5 6.2 copy-start.3
  161.5 156.9 %all-to-all-start = ((bf16[32,16,1152]{2,0,1:T(8,128)(2,1)}), bf16[32,16,1152]{2,0,1:T(8,128)(2,1)S(1)}, u32[]{:S(2)}, u32[]{:S(2)}) async-start(bf16[32,16,1152]{2,0,1:T(8,128)(2,1)} %bitcast.33), calls=%async_computation | async-start | bytes 2359296 | tf_op jit(solution)/shard_map/all_to_all | solution.py:36
  167.4 141.7 %all-gather.9.cloned.1.call-start = ((), (), s32[]{:S(2)}) async-start(), calls=%async_computation.5 | async-start | bytes 2433024 | tf_op jit(solution)/shard_map/all_gather | solution.py:31
  318.5 6.0 copy-start.2
  318.5 55.0 %all-to-all-start.1 = ((bf16[32,16,1152]{2,0,1:T(8,128)(2,1)}), bf16[32,16,1152]{2,0,1:T(8,128)(2,1)S(1)}, u32[]{:S(2)}, u32[]{:S(2)}) async-start(bf16[32,16,1152]{2,0,1:T(8,128)(2,1)} %bitcast.32), calls=%async_computation.1 | async-start | bytes 2359296 | tf_op jit(solution)/shard_map/all_to_all | solution.py:35
  324.4 248.0 %all-reduce.3.cloned.1.call-start = ((), (), s32[]{:S(2)}) async-start(), calls=%async_computation.7 | async-start | bytes 2097152 | tf_op jit(solution)/shard_map/psum | solution.py:40
  373.4 1.4 copy-start.5
  374.7 0.8 copy-start.4
  374.8 318.2 %all-gather.11.cloned.1.call-start = ((), (), s32[]{:S(2)}) async-start(), calls=%async_computation.6 | async-start | bytes 1351680 | tf_op jit(solution)/shard_map/all_gather | solution.py:46
  376.2 635.5 %reduce-scatter.2.cloned.1.call-start = ((), (), s32[]{:S(2)}) async-start(), calls=%async_computation.3 | async-start | bytes 2433024 | tf_op jit(solution)/shard_map/reduce_scatter | solution.py:50
  695.1 1.5 copy-start.1
Sparse Core Ops, SparseCore 0:
  12.3 139.8 all-gather.6
  173.1 135.9 all-gather.8
  374.9 197.4 all-reduce.2
  577.3 115.6 all-gather.10
  700.2 311.4 reduce-scatter.1
where the time goes:
time: 1020 us
  waiting for transfers between devices  959 us (94%)
  other arithmetic  21.2 us (2%)
  between operations  13.9 us (1%)
  starting transfers between devices  12.2 us (1%)
    reduce_scatter x1, waiting for transfers between devices, body(): lax.psum_scatter(jnp.einsum('tf,df->td', hidden_grad, up_weight, preferre...  313 us
    psum x1, waiting for transfers between devices, body(): pre, act_grad = lax.psum((pre_part, grad_part), 'narrow')  196 us
    all_gather x1, waiting for transfers between devices, body(): lax.all_gather(grad_out, 'wide', axis=0, tiled=True)  143 us
    all_gather x1, waiting for transfers between devices, body(): lax.all_gather(x_row, 'wide', axis=0, tiled=True)  141 us
    all_gather x1, waiting for transfers between devices, body(): lax.all_gather(x_col, 'wide', axis=1, tiled=True)  117 us
    all_to_all x1, waiting for transfers between devices, body(): lax.all_to_all(whole_x, 'narrow', split_axis=1, concat_axis=0, tiled=True)  47.7 us
  transfers between devices with their start and end apart: 7, of which 6 were waited for; matrix products, arithmetic and copies ran while one was open for 2% of the time, Pallas kernels for 0%

commit v1 on v0

v1 whole, which is shorter than its diff:
```python
import jax
import jax.numpy as jnp
from jax import lax
from jax.sharding import Mesh
from jax.sharding import PartitionSpec as P

XY = ("x", "y")


def dequant_rows(codes, exps):
    tok_count, col_count = codes.shape
    blocks = codes.astype(jnp.float32).reshape(tok_count, col_count // 32, 32)
    blocks = blocks * jnp.exp2(exps.astype(jnp.float32))[:, :, None]
    return blocks.reshape(tok_count, col_count).astype(jnp.bfloat16)


def dequant_cols(codes, exps):
    tok_count, col_count = codes.shape
    blocks = codes.astype(jnp.float32).reshape(tok_count // 32, 32, col_count)
    blocks = blocks * jnp.exp2(exps.astype(jnp.float32))[:, None, :]
    return blocks.reshape(tok_count, col_count).astype(jnp.bfloat16)


def exchange(parts, axes):
    return lax.all_to_all(parts, axes, 0, 0)


def gather(part, axes, count):
    return exchange(jnp.broadcast_to(part[None], (count,) + part.shape), axes)


def other(part, axis):
    return lax.ppermute(part, axis, [(0, 1), (1, 0)])


def body(x_row_codes, x_row_scales, x_col_codes, x_col_scales, grad_out, up_weight, down_weight):
    bf16, f32 = jnp.bfloat16, jnp.float32
    width = up_weight.shape[0]
    core = lax.axis_index("c")
    z_hi = lax.axis_index("zh")

    x_row = dequant_rows(x_row_codes, x_row_scales)
    rows = jnp.stack([x_row.reshape(16, width), grad_out.reshape(16, width)], axis=1)
    rows = jnp.broadcast_to(rows[None], (2, 16, 2, width)).reshape(32, 2, width)
    rows = exchange(rows, ("zh", "zl", "c"))

    x_cols = gather(rows[:, 0], XY, 16).reshape(512, width)
    g_cols = gather(rows[:, 1], XY, 16).reshape(512, width)

    x_col = dequant_cols(x_col_codes, x_col_scales).T
    far = other(x_col, "zh")
    x_col = jnp.where(z_hi == 0, jnp.stack([x_col, far]), jnp.stack([far, x_col]))
    x_col = gather(x_col, XY, 16).reshape(width, 512)

    def reduce_narrow(part):
        part = part.reshape(8, 2, 32, 256)
        mine = lax.dynamic_index_in_dim(part, core, 1, keepdims=False)
        theirs = other(lax.dynamic_index_in_dim(part, 1 - core, 1, keepdims=False), "c")
        return exchange((mine + theirs).astype(bf16), "zl").astype(f32).sum(axis=0)

    pre = reduce_narrow(jnp.dot(x_cols, up_weight, preferred_element_type=f32))
    act_grad = reduce_narrow(jnp.einsum("td,fd->tf", g_cols, down_weight, preferred_element_type=f32))
    positive = jnp.maximum(pre, 0.0)
    squared = (positive * positive).astype(bf16)
    hidden_grad = (act_grad * 2.0 * positive).astype(bf16)

    both = gather(jnp.stack([hidden_grad, squared]), "zl", 8)
    far = other(both, "c")
    both = jnp.where(core == 0, jnp.stack([both, far], axis=1), jnp.stack([far, both], axis=1))
    squared = both[:, :, 1].reshape(512, 256)
    hidden_grad = both[:, :, 0].reshape(32, 16, 256).transpose(1, 0, 2).reshape(512, 256)

    part = jnp.einsum("tf,df->td", hidden_grad, up_weight, preferred_element_type=f32)
    part = exchange(part.astype(bf16).reshape(16, 32, width), XY).astype(f32).sum(axis=0)
    part = part.reshape(2, 16, width)
    mine = lax.dynamic_index_in_dim(part, z_hi, 0, keepdims=False)
    theirs = other(lax.dynamic_index_in_dim(part, 1 - z_hi, 0, keepdims=False), "zh")
    input_grad = (mine + theirs).astype(bf16)

    down_grad = jnp.einsum("tf,td->fd", squared, g_cols, preferred_element_type=f32)
    up_grad = jnp.dot(x_col, hidden_grad, preferred_element_type=f32)
    return (input_grad, up_grad, down_grad)


def solution(mesh):
    mesh = Mesh(mesh.devices.reshape(4, 4, 2, 8, 2), ("x", "y", "zh", "zl", "c"))
    wide, narrow = ("x", "y", "zh"), ("zl", "c")
    in_specs = (
        P(narrow + wide, None),
        P(narrow + wide, None),
        P(None, narrow + wide),
        P(None, narrow + wide),
        P(narrow + wide, None),
        P(narrow, wide),
        P(wide, narrow),
    )
    out_specs = (P(wide, narrow), P(narrow, wide), P(wide, narrow))
    return jax.shard_map(body, mesh=mesh, in_specs=in_specs, out_specs=out_specs, check_vma=False)
```

time: 1020 us -> 212 us (0.21)
  the two profiles are of different devices: /device:TPU:1 before, /device:TPU:64 now
where the time goes in v1:
time: 212 us; the launch traced here: 211 us
  waiting for transfers between devices  95.3 us (45%)
  starting transfers between devices  58.1 us (27%)
  blocking collectives  29.5 us (14%)
  local copies, waits for them, and re-layouts  10.4 us (5%)
  other arithmetic  8.48 us (4%)
  matrix products  7.96 us (4%)
    all_to_all x7, waiting for transfers between devices, exchange(): return lax.all_to_all(parts, axes, 0, 0)  78.4 us
    all_to_all x7, starting transfers between devices, exchange(): return lax.all_to_all(parts, axes, 0, 0)  37.5 us
    all_to_all x1, blocking collectives, exchange(): return lax.all_to_all(parts, axes, 0, 0)  29.5 us
    ppermute x5, starting transfers between devices, other(): return lax.ppermute(part, axis, [(0, 1), (1, 0)])  20.7 us
    ppermute x5, waiting for transfers between devices, other(): return lax.ppermute(part, axis, [(0, 1), (1, 0)])  17 us
    broadcast_in_dim x4, local copies, waits for them, and re-layouts, gather(): return exchange(jnp.broadcast_to(part[None], (count,) + part.shape), axes)  4.55 us
  transfers between devices with their start and end apart: 12, of which 10 were waited for; matrix products, arithmetic and copies ran while one was open for 7% of the time, Pallas kernels for 0%

profile of v1, /device:TPU:64, one launch (start us, length us, event | category | flops | bytes accessed | tf_op | source)
XLA Modules:
  0.0 210.9 jit_solution(9579009224669362765)
XLA Ops:
  0.6 0.0 copy-start
  0.6 1.1 reduce.2
  1.8 0.1 stack_reshape.7
  1.9 0.7 exponential_reduce_fusion
  2.6 0.1 mul.61
  2.7 0.2 mul.62
  2.9 1.1 convert_reduce_fusion.3
  4.0 0.1 stack_reshape.6
  4.1 0.1 copy.21
  4.2 0.1 broadcast_in_dim.14
  4.3 29.5 %all_to_all.40 = bf16[32,2,1152]{2,1,0:T(2,128)(2,1)S(1)} all-to-all(bf16[32,2,1152]{2,1,0:T(2,128)(2,1)S(1)} %bitcast.80), channel_id=1, replica_groups=mesh['x'=4,'y'=4,'zh'=2,'zl'=8,'c'=2] {'zh','zl','c'}, dimensions={0} | all-to-all | bytes 294912 | tf_op jit(solution)/shard_map/all_to_all | solution.py:25
  33.8 0.2 fusion.12
  34.0 1.1 broadcast_in_dim.18
  35.1 7.0 %all-to-all-start.3 = ((bf16[16,32,1152]{2,1,0:T(8,128)(2,1)}), bf16[16,32,1152]{2,1,0:T(8,128)(2,1)S(1)}, u32[]{:S(2)}, u32[]{:S(2)}) async-start(bf16[16,32,1152]{2,1,0:T(8,128)(2,1)} %broadcast_in_dim.18), calls=%async_computation.3 | async-start | bytes 2359296 | tf_op jit(solution)/shard_map/all_to_all | solution.py:25
  42.2 19.9 %all-to-all-done.3 = bf16[16,32,1152]{2,1,0:T(8,128)(2,1)S(1)} async-done(((bf16[16,32,1152]{2,1,0:T(8,128)(2,1)}), bf16[16,32,1152]{2,1,0:T(8,128)(2,1)S(1)}, u32[]{:S(2)}, u32[]{:S(2)}) %all-to-all-start.3) | async-done | bytes 1179680 | tf_op jit(solution)/shard_map/all_to_all | solution.py:25
  62.1 1.1 broadcast_in_dim.16
  63.2 3.7 %all-to-all-start.1 = ((bf16[16,32,1152]{2,1,0:T(8,128)(2,1)}), bf16[16,32,1152]{2,1,0:T(8,128)(2,1)S(1)}, u32[]{:S(2)}, u32[]{:S(2)}) async-start(bf16[16,32,1152]{2,1,0:T(8,128)(2,1)} %broadcast_in_dim.16), calls=%async_computation.1 | async-start | bytes 2359296 | tf_op jit(solution)/shard_map/all_to_all | solution.py:25
  67.0 0.0 copy-done
  67.0 0.5 fusion
  67.5 1.9 collective-permute-start.1
  69.4 15.6 %all-to-all-done.1 = bf16[16,32,1152]{2,1,0:T(8,128)(2,1)S(1)} async-done(((bf16[16,32,1152]{2,1,0:T(8,128)(2,1)}), bf16[16,32,1152]{2,1,0:T(8,128)(2,1)S(1)}, u32[]{:S(2)}, u32[]{:S(2)}) %all-to-all-start.1) | async-done | bytes 1179680 | tf_op jit(solution)/shard_map/all_to_all | solution.py:25
  85.0 1.6 fusion.2
  86.6 1.9 collective-permute-start
  88.6 0.0 collective-permute-done.1
  88.6 1.6 fusion.4
  90.2 6.2 %all-to-all-start.4 = ((bf16[8,32,256]{2,1,0:T(8,128)(2,1)}), bf16[8,32,256]{2,1,0:T(8,128)(2,1)S(1)}, u32[]{:S(2)}, u32[]{:S(2)}) async-start(bf16[8,32,256]{2,1,0:T(8,128)(2,1)} %fusion.4), calls=%async_computation.4 | async-start | bytes 262144 | tf_op jit(solution)/shard_map/all_to_all | solution.py:25
  96.4 0.0 copy-start.4
  96.4 0.0 collective-permute-done
  96.4 1.6 fusion.5
  98.1 0.0 copy-start.3
  98.1 8.9 %all-to-all-done.4 = bf16[8,32,256]{2,1,0:T(8,128)(2,1)S(1)} async-done(((bf16[8,32,256]{2,1,0:T(8,128)(2,1)}), bf16[8,32,256]{2,1,0:T(8,128)(2,1)S(1)}, u32[]{:S(2)}, u32[]{:S(2)}) %all-to-all-start.4) | async-done | bytes 131104 | tf_op jit(solution)/shard_map/all_to_all | solution.py:25
  107.0 6.3 %all-to-all-start.2 = ((bf16[8,32,256]{2,1,0:T(8,128)(2,1)}), bf16[8,32,256]{2,1,0:T(8,128)(2,1)S(1)}, u32[]{:S(2)}, u32[]{:S(2)}) async-start(bf16[8,32,256]{2,1,0:T(8,128)(2,1)} %fusion.5), calls=%async_computation.2 | async-start | bytes 262144 | tf_op jit(solution)/shard_map/all_to_all | solution.py:25
  113.3 9.9 %all-to-all-done.2 = bf16[8,32,256]{2,1,0:T(8,128)(2,1)S(1)} async-done(((bf16[8,32,256]{2,1,0:T(8,128)(2,1)}), bf16[8,32,256]{2,1,0:T(8,128)(2,1)S(1)}, u32[]{:S(2)}, u32[]{:S(2)}) %all-to-all-start.2) | async-done | bytes 131104 | tf_op jit(solution)/shard_map/all_to_all | solution.py:25
  123.3 0.7 broadcast_in_dim.19
  124.0 6.1 %all-to-all-start.5 = ((bf16[8,2,32,256]{3,2,1,0:T(8,128)(2,1)}), bf16[8,2,32,256]{3,2,1,0:T(8,128)(2,1)S(1)}, u32[]{:S(2)}, u32[]{:S(2)}) async-start(bf16[8,2,32,256]{3,2,1,0:T(8,128)(2,1)} %broadcast_in_dim.19), calls=%async_computation.5 | async-start | bytes 524288 | tf_op jit(solution)/shard_map/all_to_all | solution.py:25
  130.1 0.0 copy-done.4
  130.2 0.1 copy.27
  130.2 0.1 mul.68
  130.4 0.2 mul.69
  130.5 0.0 copy-done.3
  130.6 6.4 %collective-permute-start.4 = (bf16[36,512]{1,0:T(8,128)(2,1)S(1)}, bf16[36,512]{1,0:T(8,128)(2,1)S(1)}, u32[]{:S(2)}, u32[]{:S(2)}) collective-permute-start(bf16[36,512]{1,0:T(8,128)(2,1)S(1)} %get-tuple-element.10), channel_id=1, source_target_pairs={{0,16},{16,0},{1,17},{17,1},{2,18},{18,2},{3,19},{19,3},{4,20},{20... | collective-permute-start | bytes 110600 | tf_op jit(solution)/shard_map/ppermute | solution.py:33
  137.0 9.7 %collective-permute-done.4 = bf16[36,512]{1,0:T(8,128)(2,1)S(1)} collective-permute-done((bf16[36,512]{1,0:T(8,128)(2,1)S(1)}, bf16[36,512]{1,0:T(8,128)(2,1)S(1)}, u32[]{:S(2)}, u32[]{:S(2)}) %collective-permute-start.4) | collective-permute-done | bytes 36896 | tf_op jit(solution)/shard_map/ppermute | solution.py:33
  146.7 0.1 copy.28
  146.8 1.2 all-to-all-done.5
  148.0 1.6 broadcast_in_dim.40
  149.6 3.7 %all-to-all-start.7 = ((bf16[16,2,36,512]{3,1,2,0:T(2,128)(2,1)}), bf16[16,2,36,512]{3,1,2,0:T(2,128)(2,1)S(1)}, u32[]{:S(2)}, u32[]{:S(2)}) async-start(bf16[16,2,36,512]{3,1,2,0:T(2,128)(2,1)} %broadcast_in_dim.40), calls=%async_computation.7 | async-start | bytes 2359296 | tf_op jit(solution)/shard_map/all_to_all | solution.py:25
  153.3 1.9 collective-permute-start.2
  155.2 1.5 collective-permute-done.2
  156.8 0.8 fusion.11
  157.6 0.1 copy.26
  157.6 1.6 convolution_convert_fusion
  159.2 11.9 %all-to-all-done.7 = bf16[16,2,36,512]{3,1,2,0:T(2,128)(2,1)S(1)} async-done(((bf16[16,2,36,512]{3,1,2,0:T(2,128)(2,1)}), bf16[16,2,36,512]{3,1,2,0:T(2,128)(2,1)S(1)}, u32[]{:S(2)}, u32[]{:S(2)}) %all-to-all-start.7) | async-done | bytes 1179680 | tf_op jit(solution)/shard_map/all_to_all | solution.py:25
  171.1 1.0 copy-done.1
  172.1 4.4 %all-to-all-start.6 = ((bf16[16,32,1152]{2,1,0:T(8,128)(2,1)}), bf16[16,32,1152]{2,1,0:T(8,128)(2,1)}, u32[]{:S(2)}, u32[]{:S(2)}) async-start(bf16[16,32,1152]{2,1,0:T(8,128)(2,1)} %bitcast.74), calls=%async_computation.6 | async-start | bytes 2359296 | tf_op jit(solution)/shard_map/all_to_all | solution.py:25
  176.5 1.5 copy.29
  178.0 1.2 reshape.134
  179.1 2.8 %fusion.13 = f32[1152,256]{1,0:T(8,128)} fusion(bf16[1152,512]{1,0:T(8,128)(2,1)} %reshape.134, bf16[512,256]{1,0:T(8,128)(2,1)S(1)} %bitcast.76), kind=kOutput, calls=%fused_computation.36 | convolution fusion | flops 301989888 | bytes 2621440 | tf_op jit(solution)/shard_map/dot_general | solution.py:81
  181.9 11.1 %all-to-all-done.6 = bf16[16,32,1152]{2,1,0:T(8,128)(2,1)} async-done(((bf16[16,32,1152]{2,1,0:T(8,128)(2,1)}), bf16[16,32,1152]{2,1,0:T(8,128)(2,1)}, u32[]{:S(2)}, u32[]{:S(2)}) %all-to-all-start.6) | async-done | bytes 1179680 | tf_op jit(solution)/shard_map/all_to_all | solution.py:25
  193.0 1.4 convert_reduce_fusion
  194.4 8.5 %collective-permute-start.3 = (f32[16,1152]{1,0:T(8,128)S(1)}, f32[16,1152]{1,0:T(8,128)S(1)}, u32[]{:S(2)}, u32[]{:S(2)}) collective-permute-start(f32[16,1152]{1,0:T(8,128)S(1)} %dynamic-slice_bitcast_fusion.2), channel_id=1, source_target_pairs={{0,16},{16,0},{1,17},{17,1},{2,18},{18,2},{3,19},{19,3},{4,20},{20... | collective-permute-start | bytes 221192 | tf_op jit(solution)/shard_map/ppermute | solution.py:33
  202.9 0.0 copy-done.2
  202.9 1.5 fusion.14
  204.5 5.8 %collective-permute-done.3 = f32[16,1152]{1,0:T(8,128)S(1)} collective-permute-done((f32[16,1152]{1,0:T(8,128)S(1)}, f32[16,1152]{1,0:T(8,128)S(1)}, u32[]{:S(2)}, u32[]{:S(2)}) %collective-permute-start.3) | collective-permute-done | bytes 73760 | tf_op jit(solution)/shard_map/ppermute | solution.py:33
  210.2 0.6 fusion.6
  (17 shorter events, 0.3 us)
Async XLA Ops:
  0.6 66.3 %copy-start = (bf16[1152,256]{1,0:T(8,128)(2,1)S(1)}, bf16[1152,256]{1,0:T(8,128)(2,1)}, u32[]{:S(2)}) copy-start(bf16[1152,256]{1,0:T(8,128)(2,1)} %param.12) | copy-start | bytes 1769476
  35.1 27.0 %all-to-all-start.3 = ((bf16[16,32,1152]{2,1,0:T(8,128)(2,1)}), bf16[16,32,1152]{2,1,0:T(8,128)(2,1)S(1)}, u32[]{:S(2)}, u32[]{:S(2)}) async-start(bf16[16,32,1152]{2,1,0:T(8,128)(2,1)} %broadcast_in_dim.18), calls=%async_computation.3 | async-start | bytes 2359296 | tf_op jit(solution)/shard_map/all_to_all | solution.py:25
  63.2 21.8 %all-to-all-start.1 = ((bf16[16,32,1152]{2,1,0:T(8,128)(2,1)}), bf16[16,32,1152]{2,1,0:T(8,128)(2,1)S(1)}, u32[]{:S(2)}, u32[]{:S(2)}) async-start(bf16[16,32,1152]{2,1,0:T(8,128)(2,1)} %broadcast_in_dim.16), calls=%async_computation.1 | async-start | bytes 2359296 | tf_op jit(solution)/shard_map/all_to_all | solution.py:25
  67.5 21.1 %collective-permute-start.1 = (f32[8,32,256]{2,1,0:T(8,128)S(1)}, f32[8,32,256]{2,1,0:T(8,128)}, u32[]{:S(2)}, u32[]{:S(2)}) collective-permute-start(f32[8,32,256]{2,1,0:T(8,128)S(1)} %dynamic-slice_bitcast_fusion), channel_id=1, source_target_pairs={{0,1},{1,0},{2,3},{3,2},{4,5},{5,4},{6,7},{7,6},{8,9},{9,8},{10,11... | collective-permute-start | bytes 786440 | tf_op jit(solution)/shard_map/ppermute | solution.py:33
  86.6 9.8 %collective-permute-start = (f32[8,32,256]{2,1,0:T(8,128)S(1)}, f32[8,32,256]{2,1,0:T(8,128)}, u32[]{:S(2)}, u32[]{:S(2)}) collective-permute-start(f32[8,32,256]{2,1,0:T(8,128)S(1)} %dynamic-slice_bitcast_fusion.1), channel_id=1, source_target_pairs={{0,1},{1,0},{2,3},{3,2},{4,5},{5,4},{6,7},{7,6},{8,9},{9,8},{10,11... | collective-permute-start | bytes 786440 | tf_op jit(solution)/shard_map/ppermute | solution.py:33
  90.2 16.8 %all-to-all-start.4 = ((bf16[8,32,256]{2,1,0:T(8,128)(2,1)}), bf16[8,32,256]{2,1,0:T(8,128)(2,1)S(1)}, u32[]{:S(2)}, u32[]{:S(2)}) async-start(bf16[8,32,256]{2,1,0:T(8,128)(2,1)} %fusion.4), calls=%async_computation.4 | async-start | bytes 262144 | tf_op jit(solution)/shard_map/all_to_all | solution.py:25
  96.4 33.7 %copy-start.4 = (s32[16,36]{1,0:T(8,128)S(1)}, s32[16,36]{1,0:T(8,128)}, u32[]{:S(2)}) copy-start(s32[16,36]{1,0:T(8,128)} %param.10) | copy-start | bytes 6916
  98.1 32.5 %copy-start.3 = (bf16[512,36]{0,1:T(8,128)(2,1)S(1)}, bf16[512,36]{0,1:T(8,128)(2,1)}, u32[]{:S(2)}) copy-start(bf16[512,36]{0,1:T(8,128)(2,1)} %param.9) | copy-start | bytes 110596
  107.0 16.2 %all-to-all-start.2 = ((bf16[8,32,256]{2,1,0:T(8,128)(2,1)}), bf16[8,32,256]{2,1,0:T(8,128)(2,1)S(1)}, u32[]{:S(2)}, u32[]{:S(2)}) async-start(bf16[8,32,256]{2,1,0:T(8,128)(2,1)} %fusion.5), calls=%async_computation.2 | async-start | bytes 262144 | tf_op jit(solution)/shard_map/all_to_all | solution.py:25
  124.0 24.0 %all-to-all-start.5 = ((bf16[8,2,32,256]{3,2,1,0:T(8,128)(2,1)}), bf16[8,2,32,256]{3,2,1,0:T(8,128)(2,1)S(1)}, u32[]{:S(2)}, u32[]{:S(2)}) async-start(bf16[8,2,32,256]{3,2,1,0:T(8,128)(2,1)} %broadcast_in_dim.19), calls=%async_computation.5 | async-start | bytes 524288 | tf_op jit(solution)/shard_map/all_to_all | solution.py:25
  130.6 16.1 %collective-permute-start.4 = (bf16[36,512]{1,0:T(8,128)(2,1)S(1)}, bf16[36,512]{1,0:T(8,128)(2,1)S(1)}, u32[]{:S(2)}, u32[]{:S(2)}) collective-permute-start(bf16[36,512]{1,0:T(8,128)(2,1)S(1)} %get-tuple-element.10), channel_id=1, source_target_pairs={{0,16},{16,0},{1,17},{17,1},{2,18},{18,2},{3,19},{19,3},{4,20},{20... | collective-permute-start | bytes 110600 | tf_op jit(solution)/shard_map/ppermute | solution.py:33
  149.6 21.5 %all-to-all-start.7 = ((bf16[16,2,36,512]{3,1,2,0:T(2,128)(2,1)}), bf16[16,2,36,512]{3,1,2,0:T(2,128)(2,1)S(1)}, u32[]{:S(2)}, u32[]{:S(2)}) async-start(bf16[16,2,36,512]{3,1,2,0:T(2,128)(2,1)} %broadcast_in_dim.40), calls=%async_computation.7 | async-start | bytes 2359296 | tf_op jit(solution)/shard_map/all_to_all | solution.py:25
  153.3 3.4 %collective-permute-start.2 = (bf16[8,2,32,256]{3,2,0,1:T(8,128)(2,1)S(1)}, bf16[8,2,32,256]{3,2,0,1:T(8,128)(2,1)S(1)}, u32[]{:S(2)}, u32[]{:S(2)}) collective-permute-start(bf16[8,2,32,256]{3,2,0,1:T(8,128)(2,1)S(1)} %copy.40), channel_id=1, source_target_pairs={{0,1},{1,0},{2,3},{3,2},{4,5},{5,4},{6,7},{7,6},{8,9},{9,8},{10,11... | collective-permute-start | bytes 786440 | tf_op jit(solution)/shard_map/ppermute | solution.py:33
  171.1 1.0 copy-start.1
  172.1 20.9 %all-to-all-start.6 = ((bf16[16,32,1152]{2,1,0:T(8,128)(2,1)}), bf16[16,32,1152]{2,1,0:T(8,128)(2,1)}, u32[]{:S(2)}, u32[]{:S(2)}) async-start(bf16[16,32,1152]{2,1,0:T(8,128)(2,1)} %bitcast.74), calls=%async_computation.6 | async-start | bytes 2359296 | tf_op jit(solution)/shard_map/all_to_all | solution.py:25
  181.9 21.0 %copy-start.2 = (bf16[8,2,1,32,256]{4,3,1,0,2:T(8,128)(2,1)S(1)}, bf16[8,2,1,32,256]{4,3,1,0,2:T(8,128)(2,1)}, u32[]{:S(2)}) copy-start(bf16[8,2,1,32,256]{4,3,1,0,2:T(8,128)(2,1)} %get-tuple-element.3) | copy-start | bytes 786436
  194.4 15.8 %collective-permute-start.3 = (f32[16,1152]{1,0:T(8,128)S(1)}, f32[16,1152]{1,0:T(8,128)S(1)}, u32[]{:S(2)}, u32[]{:S(2)}) collective-permute-start(f32[16,1152]{1,0:T(8,128)S(1)} %dynamic-slice_bitcast_fusion.2), channel_id=1, source_target_pairs={{0,16},{16,0},{1,17},{17,1},{2,18},{18,2},{3,19},{19,3},{4,20},{20... | collective-permute-start | bytes 221192 | tf_op jit(solution)/shard_map/ppermute | solution.py:33

commit v2 on v1

v2 whole, which is shorter than its diff:
```python
import jax
import jax.numpy as jnp
from jax import lax
from jax.sharding import Mesh
from jax.sharding import PartitionSpec as P

XY = ("x", "y")
WIDE = ("x", "y", "zh")
NARROW = ("zl", "c")
F32 = jnp.float32
BF16 = jnp.bfloat16


def dequant_rows(codes, exps):
    tok_count, col_count = codes.shape
    blocks = codes.astype(F32).reshape(tok_count, col_count // 32, 32)
    blocks = blocks * jnp.exp2(exps.astype(F32))[:, :, None]
    return blocks.reshape(tok_count, col_count).astype(BF16)


def dequant_cols(codes, exps):
    tok_count, col_count = codes.shape
    blocks = codes.astype(F32).reshape(tok_count // 32, 32, col_count)
    blocks = blocks * jnp.exp2(exps.astype(F32))[:, None, :]
    return blocks.reshape(tok_count, col_count).astype(BF16)


def exchange(parts, axes):
    return lax.all_to_all(parts, axes, 0, 0)


def gather(part, axes, count):
    return exchange(jnp.broadcast_to(part[None], (count,) + part.shape), axes)


def partner(part, axis):
    return lax.ppermute(part, axis, [(0, 1), (1, 0)])


def pick(parts, index, axis=0):
    return lax.dynamic_index_in_dim(parts, index, axis, keepdims=False)


def in_order(index, own, far, axis=0):
    return jnp.where(index == 0, jnp.stack([own, far], axis), jnp.stack([far, own], axis))


def partial_sums(tokens, up, down):
    width = up[0].shape[0]
    x = [tokens[:, 0, k].reshape(256, width) for k in range(2)]
    g = [tokens[:, 1, k].reshape(256, width) for k in range(2)]
    pre = sum(jnp.dot(x[k], up[k], preferred_element_type=F32) for k in range(2))
    act = sum(jnp.einsum("td,fd->tf", g[k], down[k], preferred_element_type=F32) for k in range(2))
    return jnp.stack([pre, act]), g


def nonlinear(sums):
    positive = jnp.maximum(sums[0], 0.0)
    squared = (positive * positive).astype(BF16)
    hidden_grad = (sums[1] * 2.0 * positive).astype(BF16)
    return jnp.stack([squared, hidden_grad])


def body(x_row_codes, x_row_scales, x_col_codes, x_col_scales, grad_out, up_weight, down_weight):
    width = up_weight.shape[0]
    core, z_hi = (lax.axis_index(a) for a in ("c", "zh"))

    x_col = dequant_cols(x_col_codes, x_col_scales).T
    x_col = in_order(z_hi, x_col, partner(x_col, "zh"))
    up = (up_weight, partner(up_weight, "c"))
    down = (down_weight, partner(down_weight, "c"))

    x_row = dequant_rows(x_row_codes, x_row_scales)
    rows = jnp.stack([x_row.reshape(8, 2, width), grad_out.reshape(8, 2, width)], axis=1)
    rows = jnp.where(core == 0, rows, rows[:, :, ::-1])
    rows = jnp.broadcast_to(rows[None], (2,) + rows.shape).reshape(16, 2, 2, width)
    rows = exchange(rows, ("zh", "zl"))
    rows, up, down = lax.optimization_barrier((rows, up, down))
    rows = rows.transpose(1, 2, 0, 3)

    sums, g = partial_sums(gather(rows, XY, 16), up, down)
    g = jnp.concatenate([g[0], partner(g[1], "c")])

    part = exchange(sums.reshape(2, 8, 32, 256).transpose(1, 0, 2, 3).astype(BF16), "zl")
    part = nonlinear(part.astype(F32).sum(axis=0))
    own = gather(part, "zl", 8).transpose(1, 0, 2, 3).reshape(2, 256, 256)
    far = partner(own, "c")

    squared = jnp.concatenate([own[0], far[0]])
    hidden = in_order(core, own[1], far[1])
    hidden = hidden.reshape(2, 16, 2, 8, 256).transpose(3, 0, 1, 2, 4).reshape(512, 256)

    part = jnp.einsum("tf,df->td", hidden, up_weight, preferred_element_type=F32)
    part = exchange(part.astype(BF16).reshape(16, 32, width), XY).astype(F32).sum(axis=0).reshape(2, 16, width)
    down_grad = jnp.einsum("tf,td->fd", squared, g, preferred_element_type=F32)

    part, x_col = lax.optimization_barrier((part, x_col))
    theirs = partner(pick(part, 1 - z_hi).astype(BF16), "zh")
    x_col = gather(x_col, XY, 16).reshape(width, 512)
    up_grad = jnp.dot(x_col, hidden, preferred_element_type=F32)
    input_grad = (pick(part, z_hi) + theirs.astype(F32)).astype(BF16)
    return (input_grad, up_grad, down_grad)


def solution(mesh):
    mesh = Mesh(mesh.devices.reshape(4, 4, 2, 8, 2), ("x", "y", "zh", "zl", "c"))
    in_specs = (
        P(NARROW + WIDE, None),
        P(NARROW + WIDE, None),
        P(None, NARROW + WIDE),
        P(None, NARROW + WIDE),
        P(NARROW + WIDE, None),
        P(NARROW, WIDE),
        P(WIDE, NARROW),
    )
    out_specs = (P(WIDE, NARROW), P(NARROW, WIDE), P(WIDE, NARROW))
    return jax.shard_map(body, mesh=mesh, in_specs=in_specs, out_specs=out_specs, check_vma=False)
```

time: 212 us -> 182 us (0.86)
  the two profiles are of different devices: /device:TPU:64 before, /device:TPU:1 now
where the time goes in v2:
time: 182 us; the launch traced here: 181 us
  blocking collectives  97.2 us (53%)
  starting transfers between devices  43.4 us (24%)
  waiting for transfers between devices  20.1 us (11%)
  matrix products  8.22 us (5%)
  local copies, waits for them, and re-layouts  7.66 us (4%)
  other arithmetic  3.87 us (2%)
    all_to_all x4, blocking collectives, exchange(): return lax.all_to_all(parts, axes, 0, 0)  97.2 us
    ppermute x6, starting transfers between devices, partner(): return lax.ppermute(part, axis, [(0, 1), (1, 0)])  31.6 us
    ppermute x6, waiting for transfers between devices, partner(): return lax.ppermute(part, axis, [(0, 1), (1, 0)])  15.5 us
    all_to_all x2, starting transfers between devices, exchange(): return lax.all_to_all(parts, axes, 0, 0)  11.9 us
    all_to_all x2, waiting for transfers between devices, exchange(): return lax.all_to_all(parts, axes, 0, 0)  4.63 us
  transfers between devices with their start and end apart: 8, of which 4 were waited for; matrix products, arithmetic and copies ran while one was open for 6% of the time, Pallas kernels for 0%

profile of v2, /device:TPU:1, one launch (start us, length us, event | category | flops | bytes accessed | tf_op | source)
XLA Modules:
  0.0 181.5 jit_solution(16299064833768252895)
XLA Ops:
  0.6 8.8 %collective-permute-start = (bf16[1152,256]{1,0:T(8,128)(2,1)}, bf16[1152,256]{1,0:T(8,128)(2,1)S(1)}, u32[]{:S(2)}, u32[]{:S(2)}) collective-permute-start(bf16[1152,256]{1,0:T(8,128)(2,1)} %param.12), channel_id=1, source_target_pairs={{0,1},{1,0},{2,3},{3,2},{4,5},{5,4},{6,7},{7,6},{8,9},{9,8},{10,11... | collective-permute-start | bytes 1769480 | tf_op jit(solution)/shard_map/ppermute | solution.py:37
  9.4 1.9 %collective-permute-start.1 = (bf16[256,1152]{1,0:T(8,128)(2,1)}, bf16[256,1152]{1,0:T(8,128)(2,1)S(1)}, u32[]{:S(2)}, u32[]{:S(2)}) collective-permute-start(bf16[256,1152]{1,0:T(8,128)(2,1)} %param.13), channel_id=1, source_target_pairs={{0,1},{1,0},{2,3},{3,2},{4,5},{5,4},{6,7},{7,6},{8,9},{9,8},{10,11... | collective-permute-start | bytes 1769480 | tf_op jit(solution)/shard_map/ppermute | solution.py:37
  11.4 0.7 exponential_reduce_fusion
  12.1 0.1 mul.40
  12.2 0.2 mul.41
  12.4 1.1 convert_reduce_fusion.2
  13.6 1.1 reduce.2
  14.7 0.6 rev.3
  15.3 0.1 copy.20
  15.4 0.1 broadcast_in_dim.8
  15.5 21.5 %all_to_all.30 = bf16[16,2,2,1152]{3,2,1,0:T(2,128)(2,1)S(1)} all-to-all(bf16[16,2,2,1152]{3,2,1,0:T(2,128)(2,1)S(1)} %bitcast.66), channel_id=1, replica_groups=mesh['x'=4,'y'=4,'zh'=2,'zl'=8,'c'=2] {'zh','zl'}, dimensions={0} | all-to-all | bytes 294912 | tf_op jit(solution)/shard_map/all_to_all | solution.py:29
  37.0 0.0 collective-permute-done
  37.0 0.0 collective-permute-done.1
  37.0 0.0 copy-start.2
  37.0 0.2 broadcast_in_dim.9
  37.3 0.5 copy-done.2
  37.8 32.7 %all_to_all.31 = bf16[16,2,2,16,1152]{4,3,2,1,0:T(8,128)(2,1)S(1)} all-to-all(bf16[16,2,2,16,1152]{4,3,2,1,0:T(8,128)(2,1)S(1)} %broadcast_in_dim.9), channel_id=1, replica_groups=mesh['x'=4,'y'=4,'zh'=2,'zl'=8,'c'=2] {'x','y'}, dimensions={0} | all-to-all | bytes 4718592 | tf_op jit(solution)/shard_map/all_to_all | solution.py:29
  70.5 0.0 copy-start.3
  70.5 1.0 fusion.17
  71.5 0.1 copy-done.3
  71.6 1.5 fusion.20
  73.1 0.0 copy-start
  73.1 0.3 fusion.19
  73.5 0.0 copy-done.1
  73.5 0.4 fusion.5
  73.9 0.3 copy-done
  74.2 0.3 fusion.4
  74.6 22.4 %all_to_all.32 = bf16[8,2,32,256]{3,2,1,0:T(8,128)(2,1)S(1)} all-to-all(bf16[8,2,32,256]{3,2,1,0:T(8,128)(2,1)S(1)} %maximum_bitcast_fusion), channel_id=1, replica_groups=mesh['x'=4,'y'=4,'zh'=2,'zl'=8,'c'=2] {'zl'}, dimensions={0} | all-to-all | bytes 524288 | tf_op jit(solution)/shard_map/all_to_all | solution.py:29
  97.0 20.6 %all_to_all.33 = bf16[8,2,32,256]{3,2,1,0:T(8,128)(2,1)S(1)} all-to-all(bf16[8,2,32,256]{3,2,1,0:T(8,128)(2,1)S(1)} %broadcast_in_dim.10), channel_id=1, replica_groups=mesh['x'=4,'y'=4,'zh'=2,'zl'=8,'c'=2] {'zl'}, dimensions={0} | all-to-all | bytes 524288 | tf_op jit(solution)/shard_map/all_to_all | solution.py:29
  117.6 8.0 %collective-permute-start.2 = (bf16[2,256,256]{2,1,0:T(8,128)(2,1)S(1)}, bf16[2,256,256]{2,1,0:T(8,128)(2,1)S(1)}, u32[]{:S(2)}, u32[]{:S(2)}) collective-permute-start(bf16[2,256,256]{2,1,0:T(8,128)(2,1)S(1)} %bitcast.63), channel_id=1, source_target_pairs={{0,1},{1,0},{2,3},{3,2},{4,5},{5,4},{6,7},{7,6},{8,9},{9,8},{10,11... | collective-permute-start | bytes 786440 | tf_op jit(solution)/shard_map/ppermute | solution.py:37
  125.6 0.7 fusion.18
  126.3 0.5 collective-permute-done.2
  126.8 0.7 slice_bitcast_fusion
  127.5 0.2 copy.25
  127.7 0.1 reshape.72
  127.8 1.6 convolution_convert_fusion
  129.4 0.0 copy-start.7
  129.4 0.0 copy-start.6
  129.4 4.4 %all-to-all-start.4 = ((bf16[16,32,1152]{2,1,0:T(8,128)(2,1)}), bf16[16,32,1152]{2,1,0:T(8,128)(2,1)S(1)}, u32[]{:S(2)}, u32[]{:S(2)}) async-start(bf16[16,32,1152]{2,1,0:T(8,128)(2,1)} %bitcast.16), calls=%async_computation.4 | async-start | bytes 2359296 | tf_op jit(solution)/shard_map/all_to_all | solution.py:29
  133.8 0.0 copy-done.7
  133.8 0.1 copy.26
  133.9 0.1 mul.47
  134.0 0.2 mul.48
  134.2 0.0 copy-done.6
  134.2 4.8 %collective-permute-start.3 = (bf16[36,512]{1,0:T(8,128)(2,1)S(1)}, bf16[36,512]{1,0:T(8,128)(2,1)S(1)}, u32[]{:S(2)}, u32[]{:S(2)}) collective-permute-start(bf16[36,512]{1,0:T(8,128)(2,1)S(1)} %get-tuple-element.28), channel_id=1, source_target_pairs={{0,16},{16,0},{1,17},{17,1},{2,18},{18,2},{3,19},{19,3},{4,20},{20... | collective-permute-start | bytes 110600 | tf_op jit(solution)/shard_map/ppermute | solution.py:37
  139.0 8.6 %collective-permute-done.3 = bf16[36,512]{1,0:T(8,128)(2,1)S(1)} collective-permute-done((bf16[36,512]{1,0:T(8,128)(2,1)S(1)}, bf16[36,512]{1,0:T(8,128)(2,1)S(1)}, u32[]{:S(2)}, u32[]{:S(2)}) %collective-permute-start.3) | collective-permute-done | bytes 36896 | tf_op jit(solution)/shard_map/ppermute | solution.py:37
  147.7 3.7 %collective-permute-start.5 = (bf16[256,1152]{1,0:T(8,128)(2,1)}, bf16[256,1152]{1,0:T(8,128)(2,1)}, u32[]{:S(2)}, u32[]{:S(2)}) collective-permute-start(bf16[256,1152]{1,0:T(8,128)(2,1)} %bitcast.7), channel_id=1, source_target_pairs={{0,1},{1,0},{2,3},{3,2},{4,5},{5,4},{6,7},{7,6},{8,9},{9,8},{10,11... | collective-permute-start | bytes 1769480 | tf_op jit(solution)/shard_map/ppermute | solution.py:37
  151.4 0.0 all-to-all-done.4
  151.4 0.2 convert_reduce_fusion
  151.6 0.1 copy.27
  151.7 1.6 broadcast_in_dim.11
  153.3 0.0 copy-start.4
  153.3 7.5 %all-to-all-start.5 = ((bf16[16,2,36,512]{3,1,2,0:T(2,128)(2,1)}), bf16[16,2,36,512]{3,1,2,0:T(2,128)(2,1)S(1)}, u32[]{:S(2)}, u32[]{:S(2)}) async-start(bf16[16,2,36,512]{3,1,2,0:T(2,128)(2,1)} %broadcast_in_dim.11), calls=%async_computation.5 | async-start | bytes 2359296 | tf_op jit(solution)/shard_map/all_to_all | solution.py:29
  160.8 4.4 %collective-permute-start.4 = (bf16[16,1152]{1,0:T(8,128)(2,1)S(1)}, bf16[16,1152]{1,0:T(8,128)(2,1)S(1)}, u32[]{:S(2)}, u32[]{:S(2)}) collective-permute-start(bf16[16,1152]{1,0:T(8,128)(2,1)S(1)} %fusion.11), channel_id=1, source_target_pairs={{0,16},{16,0},{1,17},{17,1},{2,18},{18,2},{3,19},{19,3},{4,20},{20... | collective-permute-start | bytes 110600 | tf_op jit(solution)/shard_map/ppermute | solution.py:37
  165.2 0.0 collective-permute-done.5
  165.2 0.0 copy-done.4
  165.2 0.0 copy-done.5
  165.2 2.6 %fusion = f32[256,1152]{1,0:T(8,128)} fusion(bf16[256,1152]{1,0:T(8,128)(2,1)} %collective-permute-done.5, bf16[256,1152]{1,0:T(8,128)(2,1)S(1)} %bitcast.60, bf16[256,256]{1,0:T(8,128)(2,1)S(1)} %copy-done.5, bf16[256,256]{1,0:T(8,128)(2,1)S(1)} %bitcast.76), kind=kOutput, calls=%fused_computation.2 | convolution fusion | flops 304873472 | bytes 2621440 | tf_op jit(solution)/shard_map/tf,td->fd/dot_general | solution.py:95
  167.8 6.4 %collective-permute-done.4 = bf16[16,1152]{1,0:T(8,128)(2,1)S(1)} collective-permute-done((bf16[16,1152]{1,0:T(8,128)(2,1)S(1)}, bf16[16,1152]{1,0:T(8,128)(2,1)S(1)}, u32[]{:S(2)}, u32[]{:S(2)}) %collective-permute-start.4) | collective-permute-done | bytes 36896 | tf_op jit(solution)/shard_map/ppermute | solution.py:37
  174.2 0.6 fusion.10
  174.8 4.6 %all-to-all-done.5 = bf16[16,2,36,512]{3,1,2,0:T(2,128)(2,1)S(1)} async-done(((bf16[16,2,36,512]{3,1,2,0:T(2,128)(2,1)}), bf16[16,2,36,512]{3,1,2,0:T(2,128)(2,1)S(1)}, u32[]{:S(2)}, u32[]{:S(2)}) %all-to-all-start.5) | async-done | bytes 1179680 | tf_op jit(solution)/shard_map/all_to_all | solution.py:29
  179.5 0.2 copy.28
  179.7 0.3 reshape.75
  180.0 1.5 fusion.21
  (19 shorter events, 0.3 us)
Async XLA Ops:
  0.6 36.3 %collective-permute-start = (bf16[1152,256]{1,0:T(8,128)(2,1)}, bf16[1152,256]{1,0:T(8,128)(2,1)S(1)}, u32[]{:S(2)}, u32[]{:S(2)}) collective-permute-start(bf16[1152,256]{1,0:T(8,128)(2,1)} %param.12), channel_id=1, source_target_pairs={{0,1},{1,0},{2,3},{3,2},{4,5},{5,4},{6,7},{7,6},{8,9},{9,8},{10,11... | collective-permute-start | bytes 1769480 | tf_op jit(solution)/shard_map/ppermute | solution.py:37
  9.4 27.5 %collective-permute-start.1 = (bf16[256,1152]{1,0:T(8,128)(2,1)}, bf16[256,1152]{1,0:T(8,128)(2,1)S(1)}, u32[]{:S(2)}, u32[]{:S(2)}) collective-permute-start(bf16[256,1152]{1,0:T(8,128)(2,1)} %param.13), channel_id=1, source_target_pairs={{0,1},{1,0},{2,3},{3,2},{4,5},{5,4},{6,7},{7,6},{8,9},{9,8},{10,11... | collective-permute-start | bytes 1769480 | tf_op jit(solution)/shard_map/ppermute | solution.py:37
  37.0 0.8 copy-start.2
  70.5 1.1 copy-start.3
  71.6 1.9 %copy-start.1 = (bf16[256,1152]{1,0:T(8,128)(2,1)S(1)}, bf16[256,1152]{1,0:T(8,128)(2,1)}, u32[]{:S(2)}) copy-start(bf16[256,1152]{1,0:T(8,128)(2,1)} %param.13) | copy-start | bytes 1769476
  73.1 1.1 copy-start
  117.6 9.1 %collective-permute-start.2 = (bf16[2,256,256]{2,1,0:T(8,128)(2,1)S(1)}, bf16[2,256,256]{2,1,0:T(8,128)(2,1)S(1)}, u32[]{:S(2)}, u32[]{:S(2)}) collective-permute-start(bf16[2,256,256]{2,1,0:T(8,128)(2,1)S(1)} %bitcast.63), channel_id=1, source_target_pairs={{0,1},{1,0},{2,3},{3,2},{4,5},{5,4},{6,7},{7,6},{8,9},{9,8},{10,11... | collective-permute-start | bytes 786440 | tf_op jit(solution)/shard_map/ppermute | solution.py:37
  129.4 4.4 %copy-start.7 = (s32[16,36]{1,0:T(8,128)S(1)}, s32[16,36]{1,0:T(8,128)}, u32[]{:S(2)}) copy-start(s32[16,36]{1,0:T(8,128)} %param.10) | copy-start | bytes 6916
  129.4 4.8 %copy-start.6 = (bf16[512,36]{0,1:T(8,128)(2,1)S(1)}, bf16[512,36]{0,1:T(8,128)(2,1)}, u32[]{:S(2)}) copy-start(bf16[512,36]{0,1:T(8,128)(2,1)} %param.9) | copy-start | bytes 110596
  129.4 22.0 %all-to-all-start.4 = ((bf16[16,32,1152]{2,1,0:T(8,128)(2,1)}), bf16[16,32,1152]{2,1,0:T(8,128)(2,1)S(1)}, u32[]{:S(2)}, u32[]{:S(2)}) async-start(bf16[16,32,1152]{2,1,0:T(8,128)(2,1)} %bitcast.16), calls=%async_computation.4 | async-start | bytes 2359296 | tf_op jit(solution)/shard_map/all_to_all | solution.py:29
  134.2 13.5 %collective-permute-start.3 = (bf16[36,512]{1,0:T(8,128)(2,1)S(1)}, bf16[36,512]{1,0:T(8,128)(2,1)S(1)}, u32[]{:S(2)}, u32[]{:S(2)}) collective-permute-start(bf16[36,512]{1,0:T(8,128)(2,1)S(1)} %get-tuple-element.28), channel_id=1, source_target_pairs={{0,16},{16,0},{1,17},{17,1},{2,18},{18,2},{3,19},{19,3},{4,20},{20... | collective-permute-start | bytes 110600 | tf_op jit(solution)/shard_map/ppermute | solution.py:37
  147.7 17.5 %collective-permute-start.5 = (bf16[256,1152]{1,0:T(8,128)(2,1)}, bf16[256,1152]{1,0:T(8,128)(2,1)}, u32[]{:S(2)}, u32[]{:S(2)}) collective-permute-start(bf16[256,1152]{1,0:T(8,128)(2,1)} %bitcast.7), channel_id=1, source_target_pairs={{0,1},{1,0},{2,3},{3,2},{4,5},{5,4},{6,7},{7,6},{8,9},{9,8},{10,11... | collective-permute-start | bytes 1769480 | tf_op jit(solution)/shard_map/ppermute | solution.py:37
  153.3 11.9 %copy-start.4 = (bf16[1,8,32,256]{3,2,1,0:T(8,128)(2,1)S(1)}, bf16[1,8,32,256]{3,2,1,0:T(8,128)(2,1)}, u32[]{:S(2)}) copy-start(bf16[1,8,32,256]{3,2,1,0:T(8,128)(2,1)} %get-tuple-element.21) | copy-start | bytes 393220
  153.3 11.9 %copy-start.5 = (bf16[256,256]{1,0:T(8,128)(2,1)S(1)}, bf16[256,256]{1,0:T(8,128)(2,1)}, u32[]{:S(2)}) copy-start(bf16[256,256]{1,0:T(8,128)(2,1)} %get-tuple-element.23) | copy-start | bytes 393220
  153.3 26.2 %all-to-all-start.5 = ((bf16[16,2,36,512]{3,1,2,0:T(2,128)(2,1)}), bf16[16,2,36,512]{3,1,2,0:T(2,128)(2,1)S(1)}, u32[]{:S(2)}, u32[]{:S(2)}) async-start(bf16[16,2,36,512]{3,1,2,0:T(2,128)(2,1)} %broadcast_in_dim.11), calls=%async_computation.5 | async-start | bytes 2359296 | tf_op jit(solution)/shard_map/all_to_all | solution.py:29
  160.8 13.4 %collective-permute-start.4 = (bf16[16,1152]{1,0:T(8,128)(2,1)S(1)}, bf16[16,1152]{1,0:T(8,128)(2,1)S(1)}, u32[]{:S(2)}, u32[]{:S(2)}) collective-permute-start(bf16[16,1152]{1,0:T(8,128)(2,1)S(1)} %fusion.11), channel_id=1, source_target_pairs={{0,16},{16,0},{1,17},{17,1},{2,18},{18,2},{3,19},{19,3},{4,20},{20... | collective-permute-start | bytes 110600 | tf_op jit(solution)/shard_map/ppermute | solution.py:37

commit v3 on v2

v3 whole, which is shorter than its diff:
```python
import jax
import jax.numpy as jnp
from jax import lax
from jax.experimental import pallas as pl
from jax.experimental.pallas import tpu as pltpu
from jax.sharding import Mesh
from jax.sharding import PartitionSpec as P

XY = ("x", "y")
WIDE = ("x", "y", "zh")
NARROW = ("zl", "c")
F32 = jnp.float32
BF16 = jnp.bfloat16


def row_kernel(codes_in, exps_in, grad_in, out_ref, codes_ref, exps_ref, grad_ref, sems):
    moves = [
        pltpu.make_async_copy(source, to, sems.at[k])
        for k, (source, to) in enumerate(((codes_in, codes_ref), (exps_in, exps_ref), (grad_in, grad_ref)))
    ]
    for move in moves:
        move.start()
    for move in moves:
        move.wait()

    span = out_ref.shape[2]
    chips, blocks = out_ref.shape[0] // 2, span // 32
    exps = jnp.concatenate([exps_ref[:, i * blocks : (i + 1) * blocks] for i in range(chips)], axis=0)
    scales = jnp.exp2(exps.astype(F32)).astype(BF16)
    block_of = lax.broadcasted_iota(jnp.int32, (blocks, span), 1) // 32
    spread = (block_of == lax.broadcasted_iota(jnp.int32, (blocks, span), 0)).astype(BF16)
    scales = jnp.dot(scales, spread, preferred_element_type=F32)
    for i in range(chips):
        codes = codes_ref[:, i * span : (i + 1) * span].astype(F32)
        grad = grad_ref[:, i * span : (i + 1) * span].astype(F32)
        pair = jnp.concatenate([codes * scales[i : i + 1], grad], axis=0).astype(BF16)
        out_ref[i] = pair
        out_ref[chips + i] = pair


def rows_of(codes, exps, grad, chips):
    return pl.pallas_call(
        row_kernel,
        out_shape=jax.ShapeDtypeStruct((2 * chips, 2, codes.shape[1] // chips), BF16),
        in_specs=[pl.BlockSpec(memory_space=pl.ANY)] * 3,
        scratch_shapes=[pltpu.VMEM(a.shape, a.dtype) for a in (codes, exps, grad)] + [pltpu.SemaphoreType.DMA((3,))],
        compiler_params=pltpu.CompilerParams(vmem_limit_bytes=60 << 20),
        cost_estimate=pl.CostEstimate(flops=2 << 20, bytes_accessed=150 << 10, transcendentals=576),
    )(codes, exps, grad)


def sums_kernel(core_ref, tokens_ref, up_ref, far_up_ref, down_ref, far_down_ref, out_ref, g_ref, far_g_ref, *sum_refs):
    xy, rows, span = tokens_ref.shape
    half, width = rows // 2, span // 2

    def products(own, far):
        def part(first, own_ref, far_ref, dims):
            total = 0.0
            for side, ref in ((own, own_ref), (far, far_ref)):
                tokens = tokens_ref[:, first : first + half, side * width : (side + 1) * width]
                total += lax.dot_general(
                    tokens.reshape(xy * half, width), ref[...], (dims, ((), ())), preferred_element_type=F32
                )
            return total

        pre = part(0, up_ref, far_up_ref, ((1,), (0,)))
        act = part(half, down_ref, far_down_ref, ((1,), (1,)))
        g = tokens_ref[:, half:].reshape(xy * half, span)
        g_ref[...] = g[:, own * width : (own + 1) * width]
        far_g_ref[...] = g[:, far * width : (far + 1) * width]
        for k in range(2):
            sum_refs[k][...] = pre[:, k * 128 : (k + 1) * 128]
            sum_refs[2 + k][...] = act[:, k * 128 : (k + 1) * 128]

    @pl.when(core_ref[0] == 0)
    def _():
        products(0, 1)

    @pl.when(core_ref[0] == 1)
    def _():
        products(1, 0)

    for i in range(8):
        for k in range(4):
            out_ref[i, k // 2, :, k % 2 * 128 : (k % 2 + 1) * 128] = sum_refs[k][pl.ds(i, 32, stride=8), :].astype(BF16)


def partial_sums(core, tokens, up, far_up, down, far_down):
    hidden = up.shape[1]
    count = tokens.shape[0] * tokens.shape[1] // 2
    vmem = pl.BlockSpec(memory_space=pltpu.VMEM)
    return pl.pallas_call(
        sums_kernel,
        out_shape=[jax.ShapeDtypeStruct((8, 2, count // 8, hidden), BF16)]
        + [jax.ShapeDtypeStruct((count, up.shape[0]), BF16)] * 2,
        in_specs=[pl.BlockSpec(memory_space=pltpu.SMEM)] + [vmem] * 5,
        out_specs=[vmem] * 3,
        scratch_shapes=[pltpu.VMEM((count, 128), F32)] * 4,
        compiler_params=pltpu.CompilerParams(vmem_limit_bytes=48 << 20),
        cost_estimate=pl.CostEstimate(flops=2 * tokens.size * hidden, bytes_accessed=5 << 20, transcendentals=0),
    )(core.reshape(1), tokens, up, far_up, down, far_down)


def share_kernel(core_ref, own_ref, far_ref, up_ref, out_ref, hidden_ref):
    @pl.when(core_ref[0] == 0)
    def _():
        hidden_ref[:, 0] = own_ref[:, 1]
        hidden_ref[:, 1] = far_ref[:, 1]

    @pl.when(core_ref[0] == 1)
    def _():
        hidden_ref[:, 0] = far_ref[:, 1]
        hidden_ref[:, 1] = own_ref[:, 1]

    hidden = hidden_ref[...].reshape(512, up_ref.shape[1])
    part = lax.dot_general(hidden, up_ref[...], (((1,), (1,)), ((), ())), preferred_element_type=F32)
    out_ref[...] = part.astype(BF16).reshape(out_ref.shape)


def shares(core, own, far, up):
    vmem = pl.BlockSpec(memory_space=pltpu.VMEM)
    return pl.pallas_call(
        share_kernel,
        out_shape=[
            jax.ShapeDtypeStruct((16, 32, up.shape[0]), BF16),
            jax.ShapeDtypeStruct((8, 2, 32, up.shape[1]), BF16),
        ],
        in_specs=[pl.BlockSpec(memory_space=pltpu.SMEM)] + [vmem] * 3,
        out_specs=[vmem] * 2,
        compiler_params=pltpu.CompilerParams(vmem_limit_bytes=32 << 20),
        cost_estimate=pl.CostEstimate(flops=1024 * up.size, bytes_accessed=3 << 20, transcendentals=0),
    )(core.reshape(1), own, far, up)


def dequant_cols(codes, exps):
    tok_count, col_count = codes.shape
    blocks = codes.astype(F32).reshape(tok_count // 32, 32, col_count)
    blocks = blocks * jnp.exp2(exps.astype(F32))[:, None, :]
    return blocks.reshape(tok_count, col_count).astype(BF16)


def exchange(parts, axes):
    return lax.all_to_all(parts, axes, 0, 0)


def gather(part, axes, count):
    return exchange(jnp.broadcast_to(part[None], (count,) + part.shape), axes)


def partner(part, axis):
    return lax.ppermute(part, axis, [(0, 1), (1, 0)])


def pick(parts, index, axis=0):
    return lax.dynamic_index_in_dim(parts, index, axis, keepdims=False)


def in_order(index, own, far, axis=0):
    return jnp.where(index == 0, jnp.stack([own, far], axis), jnp.stack([far, own], axis))


def nonlinear(sums):
    positive = jnp.maximum(sums[0], 0.0)
    squared = (positive * positive).astype(BF16)
    hidden_grad = (sums[1] * 2.0 * positive).astype(BF16)
    return jnp.stack([squared, hidden_grad])


def body(x_row_codes, x_row_scales, x_col_codes, x_col_scales, grad_out, up_weight, down_weight):
    width = up_weight.shape[0]
    core, z_hi = (lax.axis_index(a) for a in ("c", "zh"))

    rows = exchange(rows_of(x_row_codes, x_row_scales, grad_out, 8), ("zh", "zl"))
    rows = rows.transpose(1, 0, 2).reshape(32, 2 * width)

    x_col = dequant_cols(x_col_codes, x_col_scales).T
    rows, x_col, up, down = lax.optimization_barrier((rows, x_col, up_weight, down_weight))
    x_col = in_order(z_hi, x_col, partner(x_col, "zh"))
    far_up, far_down = partner(up, "c"), partner(down, "c")

    tokens = gather(rows, XY, 16)
    tokens, far_up, far_down, x_col = lax.optimization_barrier((tokens, far_up, far_down, x_col))
    sums, g, far_g = partial_sums(core, tokens, up, far_up, down, far_down)
    far_g, x_col = lax.optimization_barrier((far_g, jnp.broadcast_to(x_col[None], (16,) + x_col.shape)))
    g = jnp.concatenate([g, partner(far_g, "c")])

    part = exchange(sums, "zl").astype(F32).sum(axis=0)
    own = gather(nonlinear(part), "zl", 8)
    far = partner(own, "c")

    part, hidden = shares(core, own, far, up_weight)
    part = exchange(part, XY).astype(F32).sum(axis=0).reshape(2, 16, width)

    part, x_col = lax.optimization_barrier((part, x_col))
    theirs = partner(pick(part, 1 - z_hi).astype(BF16), "zh")
    x_col = exchange(x_col, XY).reshape(width, 512)
    up_grad = jnp.dot(x_col, hidden.reshape(512, 256), preferred_element_type=F32)
    input_grad = (pick(part, z_hi) + theirs.astype(F32)).astype(BF16)

    squared = jnp.stack([own[:, 0], far[:, 0]]).transpose(0, 2, 1, 3).reshape(512, 256)
    down_grad = jnp.einsum("tf,td->fd", squared, g, preferred_element_type=F32)
    return (input_grad, up_grad, down_grad)


def solution(mesh):
    mesh = Mesh(mesh.devices.reshape(4, 4, 2, 8, 2), ("x", "y", "zh", "zl", "c"))
    in_specs = (
        P(NARROW + WIDE, None),
        P(NARROW + WIDE, None),
        P(None, NARROW + WIDE),
        P(None, NARROW + WIDE),
        P(NARROW + WIDE, None),
        P(NARROW, WIDE),
        P(WIDE, NARROW),
    )
    out_specs = (P(WIDE, NARROW), P(NARROW, WIDE), P(WIDE, NARROW))
    return jax.shard_map(body, mesh=mesh, in_specs=in_specs, out_specs=out_specs, check_vma=False)
```

time: 182 us -> 168 us (0.923)
  blocking collectives: 97.2 us -> 41.9 us
  waiting for transfers between devices: 20.1 us -> 44 us
  starting transfers between devices: 43.4 us -> 61 us
  Pallas kernels: 0 us -> 5.74 us
  matrix products: 8.22 us -> 4.09 us
  local copies, waits for them, and re-layouts: 7.66 us -> 4.48 us
    all_to_all x4 -> x2, blocking collectives: 97.2 us -> 41.9 us  [exchange(): return lax.all_to_all(parts, axes, 0, 0)]
    all_to_all x2 -> x4, waiting for transfers between devices: 4.63 us -> 29 us  [exchange(): return lax.all_to_all(parts, axes, 0, 0)]
    all_to_all x2 -> x4, starting transfers between devices: 11.9 us -> 31.9 us  [exchange(): return lax.all_to_all(parts, axes, 0, 0)]
    pallas_call x0 -> x3, Pallas kernels: none -> 5.74 us  [the longest x1 2.22 us: partial_sums(): pl.pallas_call(sums_kernel, out_shape=[jax.ShapeDtypeStruct((8, 2, count...]
    dot_general x6 -> x1, matrix products: 5.61 us -> 1.48 us  [body(): jnp.dot(x_col, hidden.reshape(512, 256), preferred_element_type=F32)]
    ppermute x6, starting transfers between devices: 31.6 us -> 29.2 us  [partner(): return lax.ppermute(part, axis, [(0, 1), (1, 0)])]
  transfers between devices with their start and end apart: 8 -> 10, of which waited for: 4 -> 7; matrix products, arithmetic and copies ran while one was open for 6% -> 5% of each run, Pallas kernels for 0% -> 0%
where the time goes in v3:
time: 168 us; the launch traced here: 166 us
  starting transfers between devices  61 us (36%)
  waiting for transfers between devices  44 us (26%)
  blocking collectives  41.9 us (25%)
  Pallas kernels  5.74 us (3%)
  local copies, waits for them, and re-layouts  4.48 us (3%)
  matrix products  4.09 us (2%)
  other arithmetic  3.72 us (2%)
    all_to_all x2, blocking collectives, exchange(): return lax.all_to_all(parts, axes, 0, 0)  41.9 us
    all_to_all x4, starting transfers between devices, exchange(): return lax.all_to_all(parts, axes, 0, 0)  31.9 us
    ppermute x6, starting transfers between devices, partner(): return lax.ppermute(part, axis, [(0, 1), (1, 0)])  29.2 us
    all_to_all x4, waiting for transfers between devices, exchange(): return lax.all_to_all(parts, axes, 0, 0)  29 us
    ppermute x6, waiting for transfers between devices, partner(): return lax.ppermute(part, axis, [(0, 1), (1, 0)])  15 us
  transfers between devices with their start and end apart: 10, of which 7 were waited for; matrix products, arithmetic and copies ran while one was open for 5% of the time, Pallas kernels for 0%

profile of v3, /device:TPU:1, one launch (start us, length us, event | category | flops | bytes accessed | tf_op | source)
XLA Modules:
  0.0 165.9 jit_solution(16808766072882509490)
XLA Ops:
  0.6 0.0 copy-start.7
  0.6 1.9 %shard_map.94 = bf16[16,2,2304]{2,1,0:T(2,128)(2,1)} custom-call(bf16[1,18432]{1,0:T(2,128)(2,1)} %codes_in.1, s32[1,576]{1,0:T(1,128)} %exps_in.1, bf16[1,18432]{1,0:T(2,128)(2,1)} %grad_in.1), custom_call_target="tpu_custom_call" | custom-call | flops 2097152 | bytes 153600 | tf_op jit(solution)/shard_map/pallas_call | solution.py:42
  2.6 15.8 %all-to-all-start = ((bf16[16,2,2304]{2,1,0:T(2,128)(2,1)}), bf16[16,2,2304]{2,1,0:T(2,128)(2,1)S(1)}, u32[]{:S(2)}, u32[]{:S(2)}) async-start(bf16[16,2,2304]{2,1,0:T(2,128)(2,1)} %shard_map.94), calls=%async_computation | async-start | bytes 294912 | tf_op jit(solution)/shard_map/all_to_all | solution.py:143
  18.4 0.7 multiply_exponential_fusion
  19.1 0.1 copy.19
  19.2 0.1 mul.26
  19.3 0.2 mul.27
  19.5 0.0 copy-done.7
  19.5 0.6 fusion.5
  20.1 10.4 %all-to-all-done = bf16[16,2,2304]{2,1,0:T(2,128)(2,1)S(1)} async-done(((bf16[16,2,2304]{2,1,0:T(2,128)(2,1)}), bf16[16,2,2304]{2,1,0:T(2,128)(2,1)S(1)}, u32[]{:S(2)}, u32[]{:S(2)}) %all-to-all-start) | async-done | bytes 147488 | tf_op jit(solution)/shard_map/all_to_all | solution.py:143
  30.5 1.7 broadcast_in_dim.6
  32.1 0.0 copy-start.1
  32.1 0.0 copy-start
  32.1 6.9 %all-to-all-start.1 = ((bf16[16,32,2304]{2,1,0:T(8,128)(2,1)}), bf16[16,32,2304]{2,1,0:T(8,128)(2,1)S(1)}, u32[]{:S(2)}, u32[]{:S(2)}) async-start(bf16[16,32,2304]{2,1,0:T(8,128)(2,1)} %broadcast_in_dim.6), calls=%async_computation.1 | async-start | bytes 4718592 | tf_op jit(solution)/shard_map/all_to_all | solution.py:143
  39.0 0.0 copy-done.1
  39.0 6.2 %collective-permute-start = (bf16[1152,256]{1,0:T(8,128)(2,1)S(1)}, bf16[1152,256]{1,0:T(8,128)(2,1)}, u32[]{:S(2)}, u32[]{:S(2)}) collective-permute-start(bf16[1152,256]{1,0:T(8,128)(2,1)S(1)} %copy-done.1), channel_id=1, source_target_pairs={{0,1},{1,0},{2,3},{3,2},{4,5},{5,4},{6,7},{7,6},{8,9},{9,8},{10,11... | collective-permute-start | bytes 1769480 | tf_op jit(solution)/shard_map/ppermute | solution.py:151
  45.2 0.0 copy-done
  45.2 1.9 %collective-permute-start.1 = (bf16[256,1152]{1,0:T(8,128)(2,1)S(1)}, bf16[256,1152]{1,0:T(8,128)(2,1)}, u32[]{:S(2)}, u32[]{:S(2)}) collective-permute-start(bf16[256,1152]{1,0:T(8,128)(2,1)S(1)} %copy-done), channel_id=1, source_target_pairs={{0,1},{1,0},{2,3},{3,2},{4,5},{5,4},{6,7},{7,6},{8,9},{9,8},{10,11... | collective-permute-start | bytes 1769480 | tf_op jit(solution)/shard_map/ppermute | solution.py:151
  47.2 4.4 %collective-permute-start.2 = (bf16[36,512]{1,0:T(8,128)(2,1)}, bf16[36,512]{1,0:T(8,128)(2,1)}, u32[]{:S(2)}, u32[]{:S(2)}) collective-permute-start(bf16[36,512]{1,0:T(8,128)(2,1)} %fusion.5), channel_id=1, source_target_pairs={{0,16},{16,0},{1,17},{17,1},{2,18},{18,2},{3,19},{19,3},{4,20},{20... | collective-permute-start | bytes 110600 | tf_op jit(solution)/shard_map/ppermute | solution.py:151
  51.5 9.4 %collective-permute-done.2 = bf16[36,512]{1,0:T(8,128)(2,1)} collective-permute-done((bf16[36,512]{1,0:T(8,128)(2,1)}, bf16[36,512]{1,0:T(8,128)(2,1)}, u32[]{:S(2)}, u32[]{:S(2)}) %collective-permute-start.2) | collective-permute-done | bytes 36896 | tf_op jit(solution)/shard_map/ppermute | solution.py:151
  60.9 1.5 maximum_select_fusion
  62.5 0.0 collective-permute-done.far_up_ref
  62.5 0.0 collective-permute-done.1.far_down_ref
  62.5 4.1 %all-to-all-done.1.tokens_ref = bf16[16,32,2304]{2,1,0:T(8,128)(2,1)S(1)} async-done(((bf16[16,32,2304]{2,1,0:T(8,128)(2,1)}), bf16[16,32,2304]{2,1,0:T(8,128)(2,1)S(1)}, u32[]{:S(2)}, u32[]{:S(2)}) %all-to-all-start.1) | async-done | bytes 2359328 | tf_op jit(solution)/shard_map/all_to_all | solution.py:143
  66.6 2.2 %shard_map.95 = (bf16[8,2,32,256]{3,2,1,0:T(8,128)(2,1)S(1)}, bf16[256,1152]{1,0:T(8,128)(2,1)S(1)}, bf16[256,1152]{1,0:T(8,128)(2,1)S(1)}) custom-call(s32[1]{0:T(128)} %bitcast.core_ref, bf16[16,32,2304]{2,1,0:T(8,128)(2,1)S(1)} %all-to-all-done.1.tokens_ref, bf16[1152,256]{1,0:T(8,128)(2,1)S(1)} %copy-done.1, ...), custom_call_target="tpu_custom_call" | custom-call | flops 603979776 | bytes 5242880 | tf_op jit(solution)/shard_map/pallas_call | solution.py:92
  68.8 0.0 copy-start.2
  68.8 0.0 copy-start.4
  68.8 21.5 %all_to_all.30 = bf16[8,2,32,256]{3,2,1,0:T(8,128)(2,1)S(1)} all-to-all(bf16[8,2,32,256]{3,2,1,0:T(8,128)(2,1)S(1)} %get-tuple-element.27), channel_id=1, replica_groups=mesh['x'=4,'y'=4,'zh'=2,'zl'=8,'c'=2] {'zl'}, dimensions={0} | all-to-all | bytes 524288 | tf_op jit(solution)/shard_map/all_to_all | solution.py:143
  90.5 20.4 %all_to_all.31.own_ref = bf16[8,2,32,256]{3,2,1,0:T(8,128)(2,1)S(1)} all-to-all(bf16[8,2,32,256]{3,2,1,0:T(8,128)(2,1)S(1)} %broadcast_in_dim.7), channel_id=1, replica_groups=mesh['x'=4,'y'=4,'zh'=2,'zl'=8,'c'=2] {'zl'}, dimensions={0} | all-to-all | bytes 524288 | tf_op jit(solution)/shard_map/all_to_all | solution.py:143
  110.8 7.6 %collective-permute-start.3 = (bf16[8,2,32,256]{3,2,1,0:T(8,128)(2,1)S(1)}, bf16[8,2,32,256]{3,2,1,0:T(8,128)(2,1)S(1)}, u32[]{:S(2)}, u32[]{:S(2)}) collective-permute-start(bf16[8,2,32,256]{3,2,1,0:T(8,128)(2,1)S(1)} %all_to_all.31.own_ref), channel_id=1, source_target_pairs={{0,1},{1,0},{2,3},{3,2},{4,5},{5,4},{6,7},{7,6},{8,9},{9,8},{10,11... | collective-permute-start | bytes 786440 | tf_op jit(solution)/shard_map/ppermute | solution.py:151
  118.4 1.1 collective-permute-done.3.far_ref
  119.6 1.6 shard_map.96
  121.2 0.0 copy-done.2
  121.2 0.0 copy-done.4
  121.2 0.0 copy-start.6
  121.2 4.5 %all-to-all-start.4 = ((bf16[16,32,1152]{2,1,0:T(8,128)(2,1)}), bf16[16,32,1152]{2,1,0:T(8,128)(2,1)S(1)}, u32[]{:S(2)}, u32[]{:S(2)}) async-start(bf16[16,32,1152]{2,1,0:T(8,128)(2,1)} %get-tuple-element.28), calls=%async_computation.4 | async-start | bytes 2359296 | tf_op jit(solution)/shard_map/all_to_all | solution.py:143
  125.7 0.0 copy-start.5
  125.7 0.0 copy-done.6
  125.7 0.1 copy.20
  125.8 1.6 broadcast_in_dim.8
  127.4 0.0 copy-done.5
  127.4 2.6 %collective-permute-start.5 = (bf16[256,1152]{1,0:T(8,128)(2,1)S(1)}, bf16[256,1152]{1,0:T(8,128)(2,1)}, u32[]{:S(2)}, u32[]{:S(2)}) collective-permute-start(bf16[256,1152]{1,0:T(8,128)(2,1)S(1)} %copy-done.5), channel_id=1, source_target_pairs={{0,1},{1,0},{2,3},{3,2},{4,5},{5,4},{6,7},{7,6},{8,9},{9,8},{10,11... | collective-permute-start | bytes 1769480 | tf_op jit(solution)/shard_map/ppermute | solution.py:151
  130.0 12.8 %all-to-all-done.4 = bf16[16,32,1152]{2,1,0:T(8,128)(2,1)S(1)} async-done(((bf16[16,32,1152]{2,1,0:T(8,128)(2,1)}), bf16[16,32,1152]{2,1,0:T(8,128)(2,1)S(1)}, u32[]{:S(2)}, u32[]{:S(2)}) %all-to-all-start.4) | async-done | bytes 1179680 | tf_op jit(solution)/shard_map/all_to_all | solution.py:143
  142.7 0.2 convert_reduce_fusion
  142.9 4.7 %all-to-all-start.5 = ((bf16[16,2,36,512]{3,1,2,0:T(2,128)(2,1)}), bf16[16,2,36,512]{3,1,2,0:T(2,128)(2,1)S(1)}, u32[]{:S(2)}, u32[]{:S(2)}) async-start(bf16[16,2,36,512]{3,1,2,0:T(2,128)(2,1)} %broadcast_in_dim.8), calls=%async_computation.5 | async-start | bytes 2359296 | tf_op jit(solution)/shard_map/all_to_all | solution.py:143
  147.6 0.0 copy-start.3
  147.7 0.2 copy.23
  147.9 6.6 %collective-permute-start.4 = (bf16[16,1152]{1,0:T(8,128)(2,1)S(1)}, bf16[16,1152]{1,0:T(8,128)(2,1)S(1)}, u32[]{:S(2)}, u32[]{:S(2)}) collective-permute-start(bf16[16,1152]{1,0:T(8,128)(2,1)S(1)} %fusion.6), channel_id=1, source_target_pairs={{0,16},{16,0},{1,17},{17,1},{2,18},{18,2},{3,19},{19,3},{4,20},{20... | collective-permute-start | bytes 110600 | tf_op jit(solution)/shard_map/ppermute | solution.py:151
  154.4 0.0 collective-permute-done.5
  154.4 0.0 copy-done.3
  154.4 2.6 %fusion = f32[256,1152]{1,0:T(8,128)} fusion(bf16[512,256]{1,0:T(8,128)(2,1)S(1)} %bitcast.34, bf16[256,1152]{1,0:T(8,128)(2,1)} %collective-permute-done.5, bf16[256,1152]{1,0:T(8,128)(2,1)S(1)} %copy-done.3), kind=kOutput, calls=%fused_computation.1 | convolution fusion | flops 304349184 | bytes 2621440 | tf_op jit(solution)/shard_map/tf,td->fd/dot_general | solution.py:201
  157.0 4.4 %collective-permute-done.4 = bf16[16,1152]{1,0:T(8,128)(2,1)S(1)} collective-permute-done((bf16[16,1152]{1,0:T(8,128)(2,1)S(1)}, bf16[16,1152]{1,0:T(8,128)(2,1)S(1)}, u32[]{:S(2)}, u32[]{:S(2)}) %collective-permute-start.4) | collective-permute-done | bytes 36896 | tf_op jit(solution)/shard_map/ppermute | solution.py:151
  161.4 0.6 fusion.4
  162.1 1.8 %all-to-all-done.5 = bf16[16,2,36,512]{3,1,2,0:T(2,128)(2,1)S(1)} async-done(((bf16[16,2,36,512]{3,1,2,0:T(2,128)(2,1)}), bf16[16,2,36,512]{3,1,2,0:T(2,128)(2,1)S(1)}, u32[]{:S(2)}, u32[]{:S(2)}) %all-to-all-start.5) | async-done | bytes 1179680 | tf_op jit(solution)/shard_map/all_to_all | solution.py:143
  163.8 0.2 copy.21
  164.1 0.3 reshape.36
  164.4 1.5 fusion.10
  (9 shorter events, 0.2 us)
Async XLA Ops:
  0.6 18.8 %copy-start.7 = (bf16[512,36]{0,1:T(8,128)(2,1)S(1)}, bf16[512,36]{0,1:T(8,128)(2,1)}, u32[]{:S(2)}) copy-start(bf16[512,36]{0,1:T(8,128)(2,1)} %param.9) | copy-start | bytes 110596
  2.6 27.9 %all-to-all-start = ((bf16[16,2,2304]{2,1,0:T(2,128)(2,1)}), bf16[16,2,2304]{2,1,0:T(2,128)(2,1)S(1)}, u32[]{:S(2)}, u32[]{:S(2)}) async-start(bf16[16,2,2304]{2,1,0:T(2,128)(2,1)} %shard_map.94), calls=%async_computation | async-start | bytes 294912 | tf_op jit(solution)/shard_map/all_to_all | solution.py:143
  32.1 6.9 %copy-start.1 = (bf16[1152,256]{1,0:T(8,128)(2,1)S(1)}, bf16[1152,256]{1,0:T(8,128)(2,1)}, u32[]{:S(2)}) copy-start(bf16[1152,256]{1,0:T(8,128)(2,1)} %up_ref.2) | copy-start | bytes 1769476
  32.1 13.1 %copy-start = (bf16[256,1152]{1,0:T(8,128)(2,1)S(1)}, bf16[256,1152]{1,0:T(8,128)(2,1)}, u32[]{:S(2)}) copy-start(bf16[256,1152]{1,0:T(8,128)(2,1)} %down_ref) | copy-start | bytes 1769476
  32.1 34.4 %all-to-all-start.1 = ((bf16[16,32,2304]{2,1,0:T(8,128)(2,1)}), bf16[16,32,2304]{2,1,0:T(8,128)(2,1)S(1)}, u32[]{:S(2)}, u32[]{:S(2)}) async-start(bf16[16,32,2304]{2,1,0:T(8,128)(2,1)} %broadcast_in_dim.6), calls=%async_computation.1 | async-start | bytes 4718592 | tf_op jit(solution)/shard_map/all_to_all | solution.py:143
  39.0 23.4 %collective-permute-start = (bf16[1152,256]{1,0:T(8,128)(2,1)S(1)}, bf16[1152,256]{1,0:T(8,128)(2,1)}, u32[]{:S(2)}, u32[]{:S(2)}) collective-permute-start(bf16[1152,256]{1,0:T(8,128)(2,1)S(1)} %copy-done.1), channel_id=1, source_target_pairs={{0,1},{1,0},{2,3},{3,2},{4,5},{5,4},{6,7},{7,6},{8,9},{9,8},{10,11... | collective-permute-start | bytes 1769480 | tf_op jit(solution)/shard_map/ppermute | solution.py:151
  45.2 17.2 %collective-permute-start.1 = (bf16[256,1152]{1,0:T(8,128)(2,1)S(1)}, bf16[256,1152]{1,0:T(8,128)(2,1)}, u32[]{:S(2)}, u32[]{:S(2)}) collective-permute-start(bf16[256,1152]{1,0:T(8,128)(2,1)S(1)} %copy-done), channel_id=1, source_target_pairs={{0,1},{1,0},{2,3},{3,2},{4,5},{5,4},{6,7},{7,6},{8,9},{9,8},{10,11... | collective-permute-start | bytes 1769480 | tf_op jit(solution)/shard_map/ppermute | solution.py:151
  47.2 13.8 %collective-permute-start.2 = (bf16[36,512]{1,0:T(8,128)(2,1)}, bf16[36,512]{1,0:T(8,128)(2,1)}, u32[]{:S(2)}, u32[]{:S(2)}) collective-permute-start(bf16[36,512]{1,0:T(8,128)(2,1)} %fusion.5), channel_id=1, source_target_pairs={{0,16},{16,0},{1,17},{17,1},{2,18},{18,2},{3,19},{19,3},{4,20},{20... | collective-permute-start | bytes 110600 | tf_op jit(solution)/shard_map/ppermute | solution.py:151
  68.8 52.3 %copy-start.2 = (bf16[256,1152]{1,0:T(8,128)(2,1)}, bf16[256,1152]{1,0:T(8,128)(2,1)S(1)}, u32[]{:S(2)}) copy-start(bf16[256,1152]{1,0:T(8,128)(2,1)S(1)} %get-tuple-element.35) | copy-start | bytes 1769476
  68.8 52.3 %copy-start.4 = (bf16[256,1152]{1,0:T(8,128)(2,1)}, bf16[256,1152]{1,0:T(8,128)(2,1)S(1)}, u32[]{:S(2)}) copy-start(bf16[256,1152]{1,0:T(8,128)(2,1)S(1)} %get-tuple-element.36) | copy-start | bytes 1769476
  110.8 8.8 %collective-permute-start.3 = (bf16[8,2,32,256]{3,2,1,0:T(8,128)(2,1)S(1)}, bf16[8,2,32,256]{3,2,1,0:T(8,128)(2,1)S(1)}, u32[]{:S(2)}, u32[]{:S(2)}) collective-permute-start(bf16[8,2,32,256]{3,2,1,0:T(8,128)(2,1)S(1)} %all_to_all.31.own_ref), channel_id=1, source_target_pairs={{0,1},{1,0},{2,3},{3,2},{4,5},{5,4},{6,7},{7,6},{8,9},{9,8},{10,11... | collective-permute-start | bytes 786440 | tf_op jit(solution)/shard_map/ppermute | solution.py:151
  121.2 4.5 %copy-start.6 = (bf16[2,36,512]{2,1,0:T(8,128)(2,1)S(1)}, bf16[2,36,512]{2,1,0:T(8,128)(2,1)}, u32[]{:S(2)}) copy-start(bf16[2,36,512]{2,1,0:T(8,128)(2,1)} %maximum_select_fusion) | copy-start | bytes 221188
  121.2 21.6 %all-to-all-start.4 = ((bf16[16,32,1152]{2,1,0:T(8,128)(2,1)}), bf16[16,32,1152]{2,1,0:T(8,128)(2,1)S(1)}, u32[]{:S(2)}, u32[]{:S(2)}) async-start(bf16[16,32,1152]{2,1,0:T(8,128)(2,1)} %get-tuple-element.28), calls=%async_computation.4 | async-start | bytes 2359296 | tf_op jit(solution)/shard_map/all_to_all | solution.py:143
  125.7 1.7 %copy-start.5 = (bf16[256,1152]{1,0:T(8,128)(2,1)S(1)}, bf16[256,1152]{1,0:T(8,128)(2,1)}, u32[]{:S(2)}) copy-start(bf16[256,1152]{1,0:T(8,128)(2,1)} %copy-done.4) | copy-start | bytes 1769476
  127.4 27.0 %collective-permute-start.5 = (bf16[256,1152]{1,0:T(8,128)(2,1)S(1)}, bf16[256,1152]{1,0:T(8,128)(2,1)}, u32[]{:S(2)}, u32[]{:S(2)}) collective-permute-start(bf16[256,1152]{1,0:T(8,128)(2,1)S(1)} %copy-done.5), channel_id=1, source_target_pairs={{0,1},{1,0},{2,3},{3,2},{4,5},{5,4},{6,7},{7,6},{8,9},{9,8},{10,11... | collective-permute-start | bytes 1769480 | tf_op jit(solution)/shard_map/ppermute | solution.py:151
  142.9 20.9 %all-to-all-start.5 = ((bf16[16,2,36,512]{3,1,2,0:T(2,128)(2,1)}), bf16[16,2,36,512]{3,1,2,0:T(2,128)(2,1)S(1)}, u32[]{:S(2)}, u32[]{:S(2)}) async-start(bf16[16,2,36,512]{3,1,2,0:T(2,128)(2,1)} %broadcast_in_dim.8), calls=%async_computation.5 | async-start | bytes 2359296 | tf_op jit(solution)/shard_map/all_to_all | solution.py:143
  147.6 6.8 %copy-start.3 = (bf16[256,1152]{1,0:T(8,128)(2,1)S(1)}, bf16[256,1152]{1,0:T(8,128)(2,1)}, u32[]{:S(2)}) copy-start(bf16[256,1152]{1,0:T(8,128)(2,1)} %copy-done.2) | copy-start | bytes 1769476
  147.9 13.6 %collective-permute-start.4 = (bf16[16,1152]{1,0:T(8,128)(2,1)S(1)}, bf16[16,1152]{1,0:T(8,128)(2,1)S(1)}, u32[]{:S(2)}, u32[]{:S(2)}) collective-permute-start(bf16[16,1152]{1,0:T(8,128)(2,1)S(1)} %fusion.6), channel_id=1, source_target_pairs={{0,16},{16,0},{1,17},{17,1},{2,18},{18,2},{3,19},{19,3},{4,20},{20... | collective-permute-start | bytes 110600 | tf_op jit(solution)/shard_map/ppermute | solution.py:151

commit v4 on v3

--- a/solution.py
+++ b/solution.py
@@ -20,16 +20,17 @@
     ]
     for move in moves:
         move.start()
-    for move in moves:
-        move.wait()
 
     span = out_ref.shape[2]
     chips, blocks = out_ref.shape[0] // 2, span // 32
+    block_of = lax.broadcasted_iota(jnp.int32, (blocks, span), 1) // 32
+    spread = (block_of == lax.broadcasted_iota(jnp.int32, (blocks, span), 0)).astype(BF16)
+    moves[1].wait()
     exps = jnp.concatenate([exps_ref[:, i * blocks : (i + 1) * blocks] for i in range(chips)], axis=0)
     scales = jnp.exp2(exps.astype(F32)).astype(BF16)
-    block_of = lax.broadcasted_iota(jnp.int32, (blocks, span), 1) // 32
-    spread = (block_of == lax.broadcasted_iota(jnp.int32, (blocks, span), 0)).astype(BF16)
     scales = jnp.dot(scales, spread, preferred_element_type=F32)
+    moves[0].wait()
+    moves[2].wait()
     for i in range(chips):
         codes = codes_ref[:, i * span : (i + 1) * span].astype(F32)
         grad = grad_ref[:, i * span : (i + 1) * span].astype(F32)
@@ -49,65 +50,64 @@
     )(codes, exps, grad)
 
 
-def sums_kernel(core_ref, tokens_ref, up_ref, far_up_ref, down_ref, far_down_ref, out_ref, g_ref, far_g_ref, *sum_refs):
+def sums_kernel(tokens_ref, up_ref, far_up_in, down_ref, far_down_in, out_ref, g_ref, far_g_ref, *scratch):
+    far_up_ref, far_down_ref, sems = scratch
+    moves = [
+        pltpu.make_async_copy(source, to, sems.at[k])
+        for k, (source, to) in enumerate(((far_up_in, far_up_ref), (far_down_in, far_down_ref)))
+    ]
+    for move in moves:
+        move.start()
     xy, rows, span = tokens_ref.shape
     half, width = rows // 2, span // 2
-
-    def products(own, far):
-        def part(first, own_ref, far_ref, dims):
-            total = 0.0
-            for side, ref in ((own, own_ref), (far, far_ref)):
-                tokens = tokens_ref[:, first : first + half, side * width : (side + 1) * width]
-                total += lax.dot_general(
-                    tokens.reshape(xy * half, width), ref[...], (dims, ((), ())), preferred_element_type=F32
-                )
-            return total
-
-        pre = part(0, up_ref, far_up_ref, ((1,), (0,)))
-        act = part(half, down_ref, far_down_ref, ((1,), (1,)))
-        g = tokens_ref[:, half:].reshape(xy * half, span)
-        g_ref[...] = g[:, own * width : (own + 1) * width]
-        far_g_ref[...] = g[:, far * width : (far + 1) * width]
-        for k in range(2):
-            sum_refs[k][...] = pre[:, k * 128 : (k + 1) * 128]
-            sum_refs[2 + k][...] = act[:, k * 128 : (k + 1) * 128]
-
-    @pl.when(core_ref[0] == 0)
-    def _():
-        products(0, 1)
-
-    @pl.when(core_ref[0] == 1)
-    def _():
-        products(1, 0)
-
-    for i in range(8):
-        for k in range(4):
-            out_ref[i, k // 2, :, k % 2 * 128 : (k % 2 + 1) * 128] = sum_refs[k][pl.ds(i, 32, stride=8), :].astype(BF16)
-
-
-def partial_sums(core, tokens, up, far_up, down, far_down):
+    count = xy * half
+    to = lax.broadcasted_iota(jnp.int32, (count, count), 0)
+    source = lax.broadcasted_iota(jnp.int32, (count, count), 1)
+    order = (source == to % (count // 8) * 8 + to // (count // 8)).astype(BF16)
+
+    core = lax.axis_index("c")
+    own, far = (pl.ds(pl.multiple_of(side * width, 128), width) for side in (core, 1 - core))
+
+    def part(first, columns, ref, dims):
+        tokens = tokens_ref[:, first : first + half, columns].reshape(count, width)
+        return lax.dot_general(tokens, ref[...], (dims, ((), ())), preferred_element_type=F32)
+
+    pre = part(0, own, up_ref, ((1,), (0,)))
+    act = part(half, own, down_ref, ((1,), (1,)))
+    g_ref[...] = tokens_ref[:, half:, own].reshape(count, width)
+    far_g_ref[...] = tokens_ref[:, half:, far].reshape(count, width)
+    for move in moves:
+        move.wait()
+    pre += part(0, far, far_up_ref, ((1,), (0,)))
+    act += part(half, far, far_down_ref, ((1,), (1,)))
+    for k, total in enumerate((pre, act)):
+        total = jnp.dot(order, total.astype(BF16), preferred_element_type=F32)
+        out_ref[:, k] = total.astype(BF16).reshape(8, count // 8, total.shape[1])
+
+
+def partial_sums(tokens, up, far_up, down, far_down):
     hidden = up.shape[1]
     count = tokens.shape[0] * tokens.shape[1] // 2
-    vmem = pl.BlockSpec(memory_space=pltpu.VMEM)
+    vmem, anywhere = pl.BlockSpec(memory_space=pltpu.VMEM), pl.BlockSpec(memory_space=pl.ANY)
     return pl.pallas_call(
         sums_kernel,
         out_shape=[jax.ShapeDtypeStruct((8, 2, count // 8, hidden), BF16)]
         + [jax.ShapeDtypeStruct((count, up.shape[0]), BF16)] * 2,
-        in_specs=[pl.BlockSpec(memory_space=pltpu.SMEM)] + [vmem] * 5,
+        in_specs=[vmem, vmem, anywhere, vmem, anywhere],
         out_specs=[vmem] * 3,
-        scratch_shapes=[pltpu.VMEM((count, 128), F32)] * 4,
+        scratch_shapes=[pltpu.VMEM(far_up.shape, BF16), pltpu.VMEM(far_down.shape, BF16), pltpu.SemaphoreType.DMA((2,))],
         compiler_params=pltpu.CompilerParams(vmem_limit_bytes=48 << 20),
         cost_estimate=pl.CostEstimate(flops=2 * tokens.size * hidden, bytes_accessed=5 << 20, transcendentals=0),
-    )(core.reshape(1), tokens, up, far_up, down, far_down)
-
-
-def share_kernel(core_ref, own_ref, far_ref, up_ref, out_ref, hidden_ref):
-    @pl.when(core_ref[0] == 0)
+    )(tokens, up, far_up, down, far_down)
+
+
+def share_kernel(own_ref, far_ref, up_ref, out_ref, hidden_ref):
+    @pl.when(lax.axis_index("c") == 0)
     def _():
         hidden_ref[:, 0] = own_ref[:, 1]
         hidden_ref[:, 1] = far_ref[:, 1]
 
-    @pl.when(core_ref[0] == 1)
+    @pl.when(lax.axis_index("c") == 1)
     def _():
         hidden_ref[:, 0] = far_ref[:, 1]
         hidden_ref[:, 1] = own_ref[:, 1]
@@ -117,7 +117,7 @@
     out_ref[...] = part.astype(BF16).reshape(out_ref.shape)
 
 
-def shares(core, own, far, up):
+def shares(own, far, up):
     vmem = pl.BlockSpec(memory_space=pltpu.VMEM)
     return pl.pallas_call(
         share_kernel,
@@ -125,11 +125,11 @@
             jax.ShapeDtypeStruct((16, 32, up.shape[0]), BF16),
             jax.ShapeDtypeStruct((8, 2, 32, up.shape[1]), BF16),
         ],
-        in_specs=[pl.BlockSpec(memory_space=pltpu.SMEM)] + [vmem] * 3,
+        in_specs=[vmem] * 3,
         out_specs=[vmem] * 2,
         compiler_params=pltpu.CompilerParams(vmem_limit_bytes=32 << 20),
         cost_estimate=pl.CostEstimate(flops=1024 * up.size, bytes_accessed=3 << 20, transcendentals=0),
-    )(core.reshape(1), own, far, up)
+    )(own, far, up)
 
 
 def dequant_cols(codes, exps):
@@ -168,7 +168,7 @@
 
 def body(x_row_codes, x_row_scales, x_col_codes, x_col_scales, grad_out, up_weight, down_weight):
     width = up_weight.shape[0]
-    core, z_hi = (lax.axis_index(a) for a in ("c", "zh"))
+    z_hi = lax.axis_index("zh")
 
     rows = exchange(rows_of(x_row_codes, x_row_scales, grad_out, 8), ("zh", "zl"))
     rows = rows.transpose(1, 0, 2).reshape(32, 2 * width)
@@ -180,7 +180,7 @@
 
     tokens = gather(rows, XY, 16)
     tokens, far_up, far_down, x_col = lax.optimization_barrier((tokens, far_up, far_down, x_col))
-    sums, g, far_g = partial_sums(core, tokens, up, far_up, down, far_down)
+    sums, g, far_g = partial_sums(tokens, up, far_up, down, far_down)
     far_g, x_col = lax.optimization_barrier((far_g, jnp.broadcast_to(x_col[None], (16,) + x_col.shape)))
     g = jnp.concatenate([g, partner(far_g, "c")])
 
@@ -188,7 +188,7 @@
     own = gather(nonlinear(part), "zl", 8)
     far = partner(own, "c")
 
-    part, hidden = shares(core, own, far, up_weight)
+    part, hidden = shares(own, far, up_weight)
     part = exchange(part, XY).astype(F32).sum(axis=0).reshape(2, 16, width)
 
     part, x_col = lax.optimization_barrier((part, x_col))

time: 168 us -> 168 us (level)
  no operation moved by 1% of the time
where the time goes in v4:
time: 168 us; the launch traced here: 166 us
  starting transfers between devices  61 us (36%)
  waiting for transfers between devices  44 us (26%)
  blocking collectives  41.9 us (25%)
  Pallas kernels  5.64 us (3%)
  local copies, waits for them, and re-layouts  4.48 us (3%)
  matrix products  4.09 us (2%)
  other arithmetic  3.72 us (2%)
    all_to_all x2, blocking collectives, exchange(): return lax.all_to_all(parts, axes, 0, 0)  41.9 us
    all_to_all x4, starting transfers between devices, exchange(): return lax.all_to_all(parts, axes, 0, 0)  31.9 us
    ppermute x6, starting transfers between devices, partner(): return lax.ppermute(part, axis, [(0, 1), (1, 0)])  29.2 us
    all_to_all x4, waiting for transfers between devices, exchange(): return lax.all_to_all(parts, axes, 0, 0)  29 us
    ppermute x6, waiting for transfers between devices, partner(): return lax.ppermute(part, axis, [(0, 1), (1, 0)])  15 us
  transfers between devices with their start and end apart: 10, of which 7 were waited for; matrix products, arithmetic and copies ran while one was open for 5% of the time, Pallas kernels for 0%

profile of v4, /device:TPU:1, one launch (start us, length us, event | category | flops | bytes accessed | tf_op | source)
XLA Modules:
  0.0 165.8 jit_solution(8643823969305452729)
XLA Ops:
  0.6 0.0 copy-start.7
  0.6 1.8 %shard_map.94 = bf16[16,2,2304]{2,1,0:T(2,128)(2,1)} custom-call(bf16[1,18432]{1,0:T(2,128)(2,1)} %codes_in.1, s32[1,576]{1,0:T(1,128)} %exps_in.1, bf16[1,18432]{1,0:T(2,128)(2,1)} %grad_in.1), custom_call_target="tpu_custom_call" | custom-call | flops 2097152 | bytes 153600 | tf_op jit(solution)/shard_map/pallas_call | solution.py:43
  2.4 15.8 %all-to-all-start = ((bf16[16,2,2304]{2,1,0:T(2,128)(2,1)}), bf16[16,2,2304]{2,1,0:T(2,128)(2,1)S(1)}, u32[]{:S(2)}, u32[]{:S(2)}) async-start(bf16[16,2,2304]{2,1,0:T(2,128)(2,1)} %shard_map.94), calls=%async_computation | async-start | bytes 294912 | tf_op jit(solution)/shard_map/all_to_all | solution.py:143
  18.2 0.7 multiply_exponential_fusion
  18.9 0.1 copy.19
  19.0 0.1 mul.26
  19.1 0.2 mul.27
  19.3 0.0 copy-done.7
  19.3 0.6 fusion.5
  19.9 10.4 %all-to-all-done = bf16[16,2,2304]{2,1,0:T(2,128)(2,1)S(1)} async-done(((bf16[16,2,2304]{2,1,0:T(2,128)(2,1)}), bf16[16,2,2304]{2,1,0:T(2,128)(2,1)S(1)}, u32[]{:S(2)}, u32[]{:S(2)}) %all-to-all-start) | async-done | bytes 147488 | tf_op jit(solution)/shard_map/all_to_all | solution.py:143
  30.3 1.7 broadcast_in_dim.6
  32.0 0.0 copy-start.1
  32.0 0.0 copy-start
  32.0 6.9 %all-to-all-start.1 = ((bf16[16,32,2304]{2,1,0:T(8,128)(2,1)}), bf16[16,32,2304]{2,1,0:T(8,128)(2,1)S(1)}, u32[]{:S(2)}, u32[]{:S(2)}) async-start(bf16[16,32,2304]{2,1,0:T(8,128)(2,1)} %broadcast_in_dim.6), calls=%async_computation.1 | async-start | bytes 4718592 | tf_op jit(solution)/shard_map/all_to_all | solution.py:143
  38.9 0.0 copy-done.1
  38.9 6.2 %collective-permute-start = (bf16[1152,256]{1,0:T(8,128)(2,1)S(1)}, bf16[1152,256]{1,0:T(8,128)(2,1)}, u32[]{:S(2)}, u32[]{:S(2)}) collective-permute-start(bf16[1152,256]{1,0:T(8,128)(2,1)S(1)} %copy-done.1), channel_id=1, source_target_pairs={{0,1},{1,0},{2,3},{3,2},{4,5},{5,4},{6,7},{7,6},{8,9},{9,8},{10,11... | collective-permute-start | bytes 1769480 | tf_op jit(solution)/shard_map/ppermute | solution.py:151
  45.1 0.0 copy-done
  45.1 1.9 %collective-permute-start.1 = (bf16[256,1152]{1,0:T(8,128)(2,1)S(1)}, bf16[256,1152]{1,0:T(8,128)(2,1)}, u32[]{:S(2)}, u32[]{:S(2)}) collective-permute-start(bf16[256,1152]{1,0:T(8,128)(2,1)S(1)} %copy-done), channel_id=1, source_target_pairs={{0,1},{1,0},{2,3},{3,2},{4,5},{5,4},{6,7},{7,6},{8,9},{9,8},{10,11... | collective-permute-start | bytes 1769480 | tf_op jit(solution)/shard_map/ppermute | solution.py:151
  47.0 4.4 %collective-permute-start.2 = (bf16[36,512]{1,0:T(8,128)(2,1)}, bf16[36,512]{1,0:T(8,128)(2,1)}, u32[]{:S(2)}, u32[]{:S(2)}) collective-permute-start(bf16[36,512]{1,0:T(8,128)(2,1)} %fusion.5), channel_id=1, source_target_pairs={{0,16},{16,0},{1,17},{17,1},{2,18},{18,2},{3,19},{19,3},{4,20},{20... | collective-permute-start | bytes 110600 | tf_op jit(solution)/shard_map/ppermute | solution.py:151
  51.4 9.4 %collective-permute-done.2 = bf16[36,512]{1,0:T(8,128)(2,1)} collective-permute-done((bf16[36,512]{1,0:T(8,128)(2,1)}, bf16[36,512]{1,0:T(8,128)(2,1)}, u32[]{:S(2)}, u32[]{:S(2)}) %collective-permute-start.2) | collective-permute-done | bytes 36896 | tf_op jit(solution)/shard_map/ppermute | solution.py:151
  60.8 1.5 maximum_select_fusion
  62.3 0.0 collective-permute-done.far_up_in
  62.3 0.0 collective-permute-done.1.far_down_in
  62.3 4.1 %all-to-all-done.1.tokens_ref = bf16[16,32,2304]{2,1,0:T(8,128)(2,1)S(1)} async-done(((bf16[16,32,2304]{2,1,0:T(8,128)(2,1)}), bf16[16,32,2304]{2,1,0:T(8,128)(2,1)S(1)}, u32[]{:S(2)}, u32[]{:S(2)}) %all-to-all-start.1) | async-done | bytes 2359328 | tf_op jit(solution)/shard_map/all_to_all | solution.py:143
  66.4 2.3 %shard_map.95 = (bf16[8,2,32,256]{3,2,1,0:T(8,128)(2,1)S(1)}, bf16[256,1152]{1,0:T(8,128)(2,1)S(1)}, bf16[256,1152]{1,0:T(8,128)(2,1)S(1)}) custom-call(bf16[16,32,2304]{2,1,0:T(8,128)(2,1)S(1)} %all-to-all-done.1.tokens_ref, bf16[1152,256]{1,0:T(8,128)(2,1)S(1)} %copy-done.1, bf16[1152,256]{1,0:T(8,128)(2,1)} %collective-permute-done.far_up_in, ...), custom_call_target="tpu_custom_call" | custom-call | flops 603979776 | bytes 5242880 | tf_op jit(solution)/shard_map/pallas_call | solution.py:92
  68.7 0.0 copy-start.2
  68.7 0.0 copy-start.4
  68.7 21.5 %all_to_all.30 = bf16[8,2,32,256]{3,2,1,0:T(8,128)(2,1)S(1)} all-to-all(bf16[8,2,32,256]{3,2,1,0:T(8,128)(2,1)S(1)} %get-tuple-element.27), channel_id=1, replica_groups=mesh['x'=4,'y'=4,'zh'=2,'zl'=8,'c'=2] {'zl'}, dimensions={0} | all-to-all | bytes 524288 | tf_op jit(solution)/shard_map/all_to_all | solution.py:143
  90.3 20.4 %all_to_all.31.own_ref = bf16[8,2,32,256]{3,2,1,0:T(8,128)(2,1)S(1)} all-to-all(bf16[8,2,32,256]{3,2,1,0:T(8,128)(2,1)S(1)} %broadcast_in_dim.7), channel_id=1, replica_groups=mesh['x'=4,'y'=4,'zh'=2,'zl'=8,'c'=2] {'zl'}, dimensions={0} | all-to-all | bytes 524288 | tf_op jit(solution)/shard_map/all_to_all | solution.py:143
  110.7 7.6 %collective-permute-start.3 = (bf16[8,2,32,256]{3,2,1,0:T(8,128)(2,1)S(1)}, bf16[8,2,32,256]{3,2,1,0:T(8,128)(2,1)S(1)}, u32[]{:S(2)}, u32[]{:S(2)}) collective-permute-start(bf16[8,2,32,256]{3,2,1,0:T(8,128)(2,1)S(1)} %all_to_all.31.own_ref), channel_id=1, source_target_pairs={{0,1},{1,0},{2,3},{3,2},{4,5},{5,4},{6,7},{7,6},{8,9},{9,8},{10,11... | collective-permute-start | bytes 786440 | tf_op jit(solution)/shard_map/ppermute | solution.py:151
  118.3 1.1 collective-permute-done.3.far_ref
  119.5 1.6 shard_map.96
  121.1 0.0 copy-done.2
  121.1 0.0 copy-done.4
  121.1 0.0 copy-start.6
  121.1 4.5 %all-to-all-start.4 = ((bf16[16,32,1152]{2,1,0:T(8,128)(2,1)}), bf16[16,32,1152]{2,1,0:T(8,128)(2,1)S(1)}, u32[]{:S(2)}, u32[]{:S(2)}) async-start(bf16[16,32,1152]{2,1,0:T(8,128)(2,1)} %get-tuple-element.28), calls=%async_computation.4 | async-start | bytes 2359296 | tf_op jit(solution)/shard_map/all_to_all | solution.py:143
  125.6 0.0 copy-start.5
  125.6 0.0 copy-done.6
  125.6 0.1 copy.20
  125.7 1.6 broadcast_in_dim.8
  127.3 0.0 copy-done.5
  127.3 2.6 %collective-permute-start.5 = (bf16[256,1152]{1,0:T(8,128)(2,1)S(1)}, bf16[256,1152]{1,0:T(8,128)(2,1)}, u32[]{:S(2)}, u32[]{:S(2)}) collective-permute-start(bf16[256,1152]{1,0:T(8,128)(2,1)S(1)} %copy-done.5), channel_id=1, source_target_pairs={{0,1},{1,0},{2,3},{3,2},{4,5},{5,4},{6,7},{7,6},{8,9},{9,8},{10,11... | collective-permute-start | bytes 1769480 | tf_op jit(solution)/shard_map/ppermute | solution.py:151
  129.9 12.8 %all-to-all-done.4 = bf16[16,32,1152]{2,1,0:T(8,128)(2,1)S(1)} async-done(((bf16[16,32,1152]{2,1,0:T(8,128)(2,1)}), bf16[16,32,1152]{2,1,0:T(8,128)(2,1)S(1)}, u32[]{:S(2)}, u32[]{:S(2)}) %all-to-all-start.4) | async-done | bytes 1179680 | tf_op jit(solution)/shard_map/all_to_all | solution.py:143
  142.6 0.2 convert_reduce_fusion
  142.8 4.7 %all-to-all-start.5 = ((bf16[16,2,36,512]{3,1,2,0:T(2,128)(2,1)}), bf16[16,2,36,512]{3,1,2,0:T(2,128)(2,1)S(1)}, u32[]{:S(2)}, u32[]{:S(2)}) async-start(bf16[16,2,36,512]{3,1,2,0:T(2,128)(2,1)} %broadcast_in_dim.8), calls=%async_computation.5 | async-start | bytes 2359296 | tf_op jit(solution)/shard_map/all_to_all | solution.py:143
  147.5 0.0 copy-start.3
  147.6 0.2 copy.23
  147.8 6.5 %collective-permute-start.4 = (bf16[16,1152]{1,0:T(8,128)(2,1)S(1)}, bf16[16,1152]{1,0:T(8,128)(2,1)S(1)}, u32[]{:S(2)}, u32[]{:S(2)}) collective-permute-start(bf16[16,1152]{1,0:T(8,128)(2,1)S(1)} %fusion.6), channel_id=1, source_target_pairs={{0,16},{16,0},{1,17},{17,1},{2,18},{18,2},{3,19},{19,3},{4,20},{20... | collective-permute-start | bytes 110600 | tf_op jit(solution)/shard_map/ppermute | solution.py:151
  154.3 0.0 collective-permute-done.5
  154.3 0.0 copy-done.3
  154.3 2.6 %fusion = f32[256,1152]{1,0:T(8,128)} fusion(bf16[512,256]{1,0:T(8,128)(2,1)S(1)} %bitcast.33, bf16[256,1152]{1,0:T(8,128)(2,1)} %collective-permute-done.5, bf16[256,1152]{1,0:T(8,128)(2,1)S(1)} %copy-done.3), kind=kOutput, calls=%fused_computation.1 | convolution fusion | flops 304349184 | bytes 2621440 | tf_op jit(solution)/shard_map/tf,td->fd/dot_general | solution.py:201
  156.9 4.5 %collective-permute-done.4 = bf16[16,1152]{1,0:T(8,128)(2,1)S(1)} collective-permute-done((bf16[16,1152]{1,0:T(8,128)(2,1)S(1)}, bf16[16,1152]{1,0:T(8,128)(2,1)S(1)}, u32[]{:S(2)}, u32[]{:S(2)}) %collective-permute-start.4) | collective-permute-done | bytes 36896 | tf_op jit(solution)/shard_map/ppermute | solution.py:151
  161.4 0.6 fusion.4
  162.0 1.7 %all-to-all-done.5 = bf16[16,2,36,512]{3,1,2,0:T(2,128)(2,1)S(1)} async-done(((bf16[16,2,36,512]{3,1,2,0:T(2,128)(2,1)}), bf16[16,2,36,512]{3,1,2,0:T(2,128)(2,1)S(1)}, u32[]{:S(2)}, u32[]{:S(2)}) %all-to-all-start.5) | async-done | bytes 1179680 | tf_op jit(solution)/shard_map/all_to_all | solution.py:143
  163.7 0.2 copy.21
  164.0 0.3 reshape.31
  164.3 1.5 fusion.10
  (9 shorter events, 0.2 us)
Async XLA Ops:
  0.6 18.7 %copy-start.7 = (bf16[512,36]{0,1:T(8,128)(2,1)S(1)}, bf16[512,36]{0,1:T(8,128)(2,1)}, u32[]{:S(2)}) copy-start(bf16[512,36]{0,1:T(8,128)(2,1)} %param.9) | copy-start | bytes 110596
  2.4 27.9 %all-to-all-start = ((bf16[16,2,2304]{2,1,0:T(2,128)(2,1)}), bf16[16,2,2304]{2,1,0:T(2,128)(2,1)S(1)}, u32[]{:S(2)}, u32[]{:S(2)}) async-start(bf16[16,2,2304]{2,1,0:T(2,128)(2,1)} %shard_map.94), calls=%async_computation | async-start | bytes 294912 | tf_op jit(solution)/shard_map/all_to_all | solution.py:143
  32.0 6.9 %copy-start.1 = (bf16[1152,256]{1,0:T(8,128)(2,1)S(1)}, bf16[1152,256]{1,0:T(8,128)(2,1)}, u32[]{:S(2)}) copy-start(bf16[1152,256]{1,0:T(8,128)(2,1)} %up_ref.2) | copy-start | bytes 1769476
  32.0 13.1 %copy-start = (bf16[256,1152]{1,0:T(8,128)(2,1)S(1)}, bf16[256,1152]{1,0:T(8,128)(2,1)}, u32[]{:S(2)}) copy-start(bf16[256,1152]{1,0:T(8,128)(2,1)} %down_ref) | copy-start | bytes 1769476
  32.0 34.4 %all-to-all-start.1 = ((bf16[16,32,2304]{2,1,0:T(8,128)(2,1)}), bf16[16,32,2304]{2,1,0:T(8,128)(2,1)S(1)}, u32[]{:S(2)}, u32[]{:S(2)}) async-start(bf16[16,32,2304]{2,1,0:T(8,128)(2,1)} %broadcast_in_dim.6), calls=%async_computation.1 | async-start | bytes 4718592 | tf_op jit(solution)/shard_map/all_to_all | solution.py:143
  38.9 23.4 %collective-permute-start = (bf16[1152,256]{1,0:T(8,128)(2,1)S(1)}, bf16[1152,256]{1,0:T(8,128)(2,1)}, u32[]{:S(2)}, u32[]{:S(2)}) collective-permute-start(bf16[1152,256]{1,0:T(8,128)(2,1)S(1)} %copy-done.1), channel_id=1, source_target_pairs={{0,1},{1,0},{2,3},{3,2},{4,5},{5,4},{6,7},{7,6},{8,9},{9,8},{10,11... | collective-permute-start | bytes 1769480 | tf_op jit(solution)/shard_map/ppermute | solution.py:151
  45.1 17.2 %collective-permute-start.1 = (bf16[256,1152]{1,0:T(8,128)(2,1)S(1)}, bf16[256,1152]{1,0:T(8,128)(2,1)}, u32[]{:S(2)}, u32[]{:S(2)}) collective-permute-start(bf16[256,1152]{1,0:T(8,128)(2,1)S(1)} %copy-done), channel_id=1, source_target_pairs={{0,1},{1,0},{2,3},{3,2},{4,5},{5,4},{6,7},{7,6},{8,9},{9,8},{10,11... | collective-permute-start | bytes 1769480 | tf_op jit(solution)/shard_map/ppermute | solution.py:151
  47.0 13.8 %collective-permute-start.2 = (bf16[36,512]{1,0:T(8,128)(2,1)}, bf16[36,512]{1,0:T(8,128)(2,1)}, u32[]{:S(2)}, u32[]{:S(2)}) collective-permute-start(bf16[36,512]{1,0:T(8,128)(2,1)} %fusion.5), channel_id=1, source_target_pairs={{0,16},{16,0},{1,17},{17,1},{2,18},{18,2},{3,19},{19,3},{4,20},{20... | collective-permute-start | bytes 110600 | tf_op jit(solution)/shard_map/ppermute | solution.py:151
  68.7 52.3 %copy-start.2 = (bf16[256,1152]{1,0:T(8,128)(2,1)}, bf16[256,1152]{1,0:T(8,128)(2,1)S(1)}, u32[]{:S(2)}) copy-start(bf16[256,1152]{1,0:T(8,128)(2,1)S(1)} %get-tuple-element.35) | copy-start | bytes 1769476
  68.7 52.3 %copy-start.4 = (bf16[256,1152]{1,0:T(8,128)(2,1)}, bf16[256,1152]{1,0:T(8,128)(2,1)S(1)}, u32[]{:S(2)}) copy-start(bf16[256,1152]{1,0:T(8,128)(2,1)S(1)} %get-tuple-element.36) | copy-start | bytes 1769476
  110.7 8.8 %collective-permute-start.3 = (bf16[8,2,32,256]{3,2,1,0:T(8,128)(2,1)S(1)}, bf16[8,2,32,256]{3,2,1,0:T(8,128)(2,1)S(1)}, u32[]{:S(2)}, u32[]{:S(2)}) collective-permute-start(bf16[8,2,32,256]{3,2,1,0:T(8,128)(2,1)S(1)} %all_to_all.31.own_ref), channel_id=1, source_target_pairs={{0,1},{1,0},{2,3},{3,2},{4,5},{5,4},{6,7},{7,6},{8,9},{9,8},{10,11... | collective-permute-start | bytes 786440 | tf_op jit(solution)/shard_map/ppermute | solution.py:151
  121.1 4.5 %copy-start.6 = (bf16[2,36,512]{2,1,0:T(8,128)(2,1)S(1)}, bf16[2,36,512]{2,1,0:T(8,128)(2,1)}, u32[]{:S(2)}) copy-start(bf16[2,36,512]{2,1,0:T(8,128)(2,1)} %maximum_select_fusion) | copy-start | bytes 221188
  121.1 21.6 %all-to-all-start.4 = ((bf16[16,32,1152]{2,1,0:T(8,128)(2,1)}), bf16[16,32,1152]{2,1,0:T(8,128)(2,1)S(1)}, u32[]{:S(2)}, u32[]{:S(2)}) async-start(bf16[16,32,1152]{2,1,0:T(8,128)(2,1)} %get-tuple-element.28), calls=%async_computation.4 | async-start | bytes 2359296 | tf_op jit(solution)/shard_map/all_to_all | solution.py:143
  125.6 1.7 %copy-start.5 = (bf16[256,1152]{1,0:T(8,128)(2,1)S(1)}, bf16[256,1152]{1,0:T(8,128)(2,1)}, u32[]{:S(2)}) copy-start(bf16[256,1152]{1,0:T(8,128)(2,1)} %copy-done.4) | copy-start | bytes 1769476
  127.3 27.0 %collective-permute-start.5 = (bf16[256,1152]{1,0:T(8,128)(2,1)S(1)}, bf16[256,1152]{1,0:T(8,128)(2,1)}, u32[]{:S(2)}, u32[]{:S(2)}) collective-permute-start(bf16[256,1152]{1,0:T(8,128)(2,1)S(1)} %copy-done.5), channel_id=1, source_target_pairs={{0,1},{1,0},{2,3},{3,2},{4,5},{5,4},{6,7},{7,6},{8,9},{9,8},{10,11... | collective-permute-start | bytes 1769480 | tf_op jit(solution)/shard_map/ppermute | solution.py:151
  142.8 20.9 %all-to-all-start.5 = ((bf16[16,2,36,512]{3,1,2,0:T(2,128)(2,1)}), bf16[16,2,36,512]{3,1,2,0:T(2,128)(2,1)S(1)}, u32[]{:S(2)}, u32[]{:S(2)}) async-start(bf16[16,2,36,512]{3,1,2,0:T(2,128)(2,1)} %broadcast_in_dim.8), calls=%async_computation.5 | async-start | bytes 2359296 | tf_op jit(solution)/shard_map/all_to_all | solution.py:143
  147.5 6.8 %copy-start.3 = (bf16[256,1152]{1,0:T(8,128)(2,1)S(1)}, bf16[256,1152]{1,0:T(8,128)(2,1)}, u32[]{:S(2)}) copy-start(bf16[256,1152]{1,0:T(8,128)(2,1)} %copy-done.2) | copy-start | bytes 1769476
  147.8 13.6 %collective-permute-start.4 = (bf16[16,1152]{1,0:T(8,128)(2,1)S(1)}, bf16[16,1152]{1,0:T(8,128)(2,1)S(1)}, u32[]{:S(2)}, u32[]{:S(2)}) collective-permute-start(bf16[16,1152]{1,0:T(8,128)(2,1)S(1)} %fusion.6), channel_id=1, source_target_pairs={{0,16},{16,0},{1,17},{17,1},{2,18},{18,2},{3,19},{19,3},{4,20},{20... | collective-permute-start | bytes 110600 | tf_op jit(solution)/shard_map/ppermute | solution.py:151

commit v5 on v4

--- a/solution.py
+++ b/solution.py
@@ -102,15 +102,9 @@
 
 
 def share_kernel(own_ref, far_ref, up_ref, out_ref, hidden_ref):
-    @pl.when(lax.axis_index("c") == 0)
-    def _():
-        hidden_ref[:, 0] = own_ref[:, 1]
-        hidden_ref[:, 1] = far_ref[:, 1]
-
-    @pl.when(lax.axis_index("c") == 1)
-    def _():
-        hidden_ref[:, 0] = far_ref[:, 1]
-        hidden_ref[:, 1] = own_ref[:, 1]
+    core = lax.axis_index("c")
+    hidden_ref[:, core] = own_ref[:, 1]
+    hidden_ref[:, 1 - core] = far_ref[:, 1]
 
     hidden = hidden_ref[...].reshape(512, up_ref.shape[1])
     part = lax.dot_general(hidden, up_ref[...], (((1,), (1,)), ((), ())), preferred_element_type=F32)

time: 168 us -> 168 us (level)
  no operation moved by 1% of the time
where the time goes in v5:
time: 168 us; the launch traced here: 166 us
  starting transfers between devices  61 us (36%)
  waiting for transfers between devices  44 us (26%)
  blocking collectives  41.9 us (25%)
  Pallas kernels  5.62 us (3%)
  local copies, waits for them, and re-layouts  4.48 us (3%)
  matrix products  4.09 us (2%)
  other arithmetic  3.72 us (2%)
    all_to_all x2, blocking collectives, exchange(): return lax.all_to_all(parts, axes, 0, 0)  41.9 us
    all_to_all x4, starting transfers between devices, exchange(): return lax.all_to_all(parts, axes, 0, 0)  31.9 us
    ppermute x6, starting transfers between devices, partner(): return lax.ppermute(part, axis, [(0, 1), (1, 0)])  29.1 us
    all_to_all x4, waiting for transfers between devices, exchange(): return lax.all_to_all(parts, axes, 0, 0)  29.1 us
    ppermute x6, waiting for transfers between devices, partner(): return lax.ppermute(part, axis, [(0, 1), (1, 0)])  15 us
  transfers between devices with their start and end apart: 10, of which 7 were waited for; matrix products, arithmetic and copies ran while one was open for 5% of the time, Pallas kernels for 0%

profile of v5, /device:TPU:1, one launch (start us, length us, event | category | flops | bytes accessed | tf_op | source)
XLA Modules:
  0.0 165.8 jit_solution(6004209591132037386)
XLA Ops:
  0.6 0.0 copy-start.7
  0.6 1.8 %shard_map.94 = bf16[16,2,2304]{2,1,0:T(2,128)(2,1)} custom-call(bf16[1,18432]{1,0:T(2,128)(2,1)} %codes_in.1, s32[1,576]{1,0:T(1,128)} %exps_in.1, bf16[1,18432]{1,0:T(2,128)(2,1)} %grad_in.1), custom_call_target="tpu_custom_call" | custom-call | flops 2097152 | bytes 153600 | tf_op jit(solution)/shard_map/pallas_call | solution.py:43
  2.4 15.8 %all-to-all-start = ((bf16[16,2,2304]{2,1,0:T(2,128)(2,1)}), bf16[16,2,2304]{2,1,0:T(2,128)(2,1)S(1)}, u32[]{:S(2)}, u32[]{:S(2)}) async-start(bf16[16,2,2304]{2,1,0:T(2,128)(2,1)} %shard_map.94), calls=%async_computation | async-start | bytes 294912 | tf_op jit(solution)/shard_map/all_to_all | solution.py:137
  18.2 0.7 multiply_exponential_fusion
  18.9 0.1 copy.19
  19.0 0.1 mul.26
  19.1 0.2 mul.27
  19.3 0.0 copy-done.7
  19.3 0.6 fusion.5
  19.9 10.4 %all-to-all-done = bf16[16,2,2304]{2,1,0:T(2,128)(2,1)S(1)} async-done(((bf16[16,2,2304]{2,1,0:T(2,128)(2,1)}), bf16[16,2,2304]{2,1,0:T(2,128)(2,1)S(1)}, u32[]{:S(2)}, u32[]{:S(2)}) %all-to-all-start) | async-done | bytes 147488 | tf_op jit(solution)/shard_map/all_to_all | solution.py:137
  30.3 1.7 broadcast_in_dim.6
  32.0 0.0 copy-start.1
  32.0 0.0 copy-start
  32.0 6.9 %all-to-all-start.1 = ((bf16[16,32,2304]{2,1,0:T(8,128)(2,1)}), bf16[16,32,2304]{2,1,0:T(8,128)(2,1)S(1)}, u32[]{:S(2)}, u32[]{:S(2)}) async-start(bf16[16,32,2304]{2,1,0:T(8,128)(2,1)} %broadcast_in_dim.6), calls=%async_computation.1 | async-start | bytes 4718592 | tf_op jit(solution)/shard_map/all_to_all | solution.py:137
  38.9 0.0 copy-done.1
  38.9 6.2 %collective-permute-start = (bf16[1152,256]{1,0:T(8,128)(2,1)S(1)}, bf16[1152,256]{1,0:T(8,128)(2,1)}, u32[]{:S(2)}, u32[]{:S(2)}) collective-permute-start(bf16[1152,256]{1,0:T(8,128)(2,1)S(1)} %copy-done.1), channel_id=1, source_target_pairs={{0,1},{1,0},{2,3},{3,2},{4,5},{5,4},{6,7},{7,6},{8,9},{9,8},{10,11... | collective-permute-start | bytes 1769480 | tf_op jit(solution)/shard_map/ppermute | solution.py:145
  45.1 0.0 copy-done
  45.1 1.9 %collective-permute-start.1 = (bf16[256,1152]{1,0:T(8,128)(2,1)S(1)}, bf16[256,1152]{1,0:T(8,128)(2,1)}, u32[]{:S(2)}, u32[]{:S(2)}) collective-permute-start(bf16[256,1152]{1,0:T(8,128)(2,1)S(1)} %copy-done), channel_id=1, source_target_pairs={{0,1},{1,0},{2,3},{3,2},{4,5},{5,4},{6,7},{7,6},{8,9},{9,8},{10,11... | collective-permute-start | bytes 1769480 | tf_op jit(solution)/shard_map/ppermute | solution.py:145
  47.0 4.4 %collective-permute-start.2 = (bf16[36,512]{1,0:T(8,128)(2,1)}, bf16[36,512]{1,0:T(8,128)(2,1)}, u32[]{:S(2)}, u32[]{:S(2)}) collective-permute-start(bf16[36,512]{1,0:T(8,128)(2,1)} %fusion.5), channel_id=1, source_target_pairs={{0,16},{16,0},{1,17},{17,1},{2,18},{18,2},{3,19},{19,3},{4,20},{20... | collective-permute-start | bytes 110600 | tf_op jit(solution)/shard_map/ppermute | solution.py:145
  51.4 9.4 %collective-permute-done.2 = bf16[36,512]{1,0:T(8,128)(2,1)} collective-permute-done((bf16[36,512]{1,0:T(8,128)(2,1)}, bf16[36,512]{1,0:T(8,128)(2,1)}, u32[]{:S(2)}, u32[]{:S(2)}) %collective-permute-start.2) | collective-permute-done | bytes 36896 | tf_op jit(solution)/shard_map/ppermute | solution.py:145
  60.8 1.5 maximum_select_fusion
  62.3 0.0 collective-permute-done.far_up_in
  62.3 0.0 collective-permute-done.1.far_down_in
  62.3 4.1 %all-to-all-done.1.tokens_ref = bf16[16,32,2304]{2,1,0:T(8,128)(2,1)S(1)} async-done(((bf16[16,32,2304]{2,1,0:T(8,128)(2,1)}), bf16[16,32,2304]{2,1,0:T(8,128)(2,1)S(1)}, u32[]{:S(2)}, u32[]{:S(2)}) %all-to-all-start.1) | async-done | bytes 2359328 | tf_op jit(solution)/shard_map/all_to_all | solution.py:137
  66.4 2.3 %shard_map.95 = (bf16[8,2,32,256]{3,2,1,0:T(8,128)(2,1)S(1)}, bf16[256,1152]{1,0:T(8,128)(2,1)S(1)}, bf16[256,1152]{1,0:T(8,128)(2,1)S(1)}) custom-call(bf16[16,32,2304]{2,1,0:T(8,128)(2,1)S(1)} %all-to-all-done.1.tokens_ref, bf16[1152,256]{1,0:T(8,128)(2,1)S(1)} %copy-done.1, bf16[1152,256]{1,0:T(8,128)(2,1)} %collective-permute-done.far_up_in, ...), custom_call_target="tpu_custom_call" | custom-call | flops 603979776 | bytes 5242880 | tf_op jit(solution)/shard_map/pallas_call | solution.py:92
  68.7 0.0 copy-start.2
  68.7 0.0 copy-start.4
  68.7 21.5 %all_to_all.30 = bf16[8,2,32,256]{3,2,1,0:T(8,128)(2,1)S(1)} all-to-all(bf16[8,2,32,256]{3,2,1,0:T(8,128)(2,1)S(1)} %get-tuple-element.27), channel_id=1, replica_groups=mesh['x'=4,'y'=4,'zh'=2,'zl'=8,'c'=2] {'zl'}, dimensions={0} | all-to-all | bytes 524288 | tf_op jit(solution)/shard_map/all_to_all | solution.py:137
  90.3 20.4 %all_to_all.31.own_ref = bf16[8,2,32,256]{3,2,1,0:T(8,128)(2,1)S(1)} all-to-all(bf16[8,2,32,256]{3,2,1,0:T(8,128)(2,1)S(1)} %broadcast_in_dim.7), channel_id=1, replica_groups=mesh['x'=4,'y'=4,'zh'=2,'zl'=8,'c'=2] {'zl'}, dimensions={0} | all-to-all | bytes 524288 | tf_op jit(solution)/shard_map/all_to_all | solution.py:137
  110.7 7.6 %collective-permute-start.3 = (bf16[8,2,32,256]{3,2,1,0:T(8,128)(2,1)S(1)}, bf16[8,2,32,256]{3,2,1,0:T(8,128)(2,1)S(1)}, u32[]{:S(2)}, u32[]{:S(2)}) collective-permute-start(bf16[8,2,32,256]{3,2,1,0:T(8,128)(2,1)S(1)} %all_to_all.31.own_ref), channel_id=1, source_target_pairs={{0,1},{1,0},{2,3},{3,2},{4,5},{5,4},{6,7},{7,6},{8,9},{9,8},{10,11... | collective-permute-start | bytes 786440 | tf_op jit(solution)/shard_map/ppermute | solution.py:145
  118.3 1.1 collective-permute-done.3.far_ref
  119.5 1.6 shard_map.96
  121.0 0.0 copy-done.2
  121.0 0.0 copy-done.4
  121.0 0.0 copy-start.6
  121.0 4.5 %all-to-all-start.4 = ((bf16[16,32,1152]{2,1,0:T(8,128)(2,1)}), bf16[16,32,1152]{2,1,0:T(8,128)(2,1)S(1)}, u32[]{:S(2)}, u32[]{:S(2)}) async-start(bf16[16,32,1152]{2,1,0:T(8,128)(2,1)} %get-tuple-element.28), calls=%async_computation.4 | async-start | bytes 2359296 | tf_op jit(solution)/shard_map/all_to_all | solution.py:137
  125.6 0.0 copy-start.5
  125.6 0.0 copy-done.6
  125.6 0.1 copy.20
  125.7 1.6 broadcast_in_dim.8
  127.3 0.0 copy-done.5
  127.3 2.6 %collective-permute-start.5 = (bf16[256,1152]{1,0:T(8,128)(2,1)S(1)}, bf16[256,1152]{1,0:T(8,128)(2,1)}, u32[]{:S(2)}, u32[]{:S(2)}) collective-permute-start(bf16[256,1152]{1,0:T(8,128)(2,1)S(1)} %copy-done.5), channel_id=1, source_target_pairs={{0,1},{1,0},{2,3},{3,2},{4,5},{5,4},{6,7},{7,6},{8,9},{9,8},{10,11... | collective-permute-start | bytes 1769480 | tf_op jit(solution)/shard_map/ppermute | solution.py:145
  129.9 12.8 %all-to-all-done.4 = bf16[16,32,1152]{2,1,0:T(8,128)(2,1)S(1)} async-done(((bf16[16,32,1152]{2,1,0:T(8,128)(2,1)}), bf16[16,32,1152]{2,1,0:T(8,128)(2,1)S(1)}, u32[]{:S(2)}, u32[]{:S(2)}) %all-to-all-start.4) | async-done | bytes 1179680 | tf_op jit(solution)/shard_map/all_to_all | solution.py:137
  142.6 0.2 convert_reduce_fusion
  142.8 4.7 %all-to-all-start.5 = ((bf16[16,2,36,512]{3,1,2,0:T(2,128)(2,1)}), bf16[16,2,36,512]{3,1,2,0:T(2,128)(2,1)S(1)}, u32[]{:S(2)}, u32[]{:S(2)}) async-start(bf16[16,2,36,512]{3,1,2,0:T(2,128)(2,1)} %broadcast_in_dim.8), calls=%async_computation.5 | async-start | bytes 2359296 | tf_op jit(solution)/shard_map/all_to_all | solution.py:137
  147.5 0.0 copy-start.3
  147.6 0.2 copy.23
  147.7 6.5 %collective-permute-start.4 = (bf16[16,1152]{1,0:T(8,128)(2,1)S(1)}, bf16[16,1152]{1,0:T(8,128)(2,1)S(1)}, u32[]{:S(2)}, u32[]{:S(2)}) collective-permute-start(bf16[16,1152]{1,0:T(8,128)(2,1)S(1)} %fusion.6), channel_id=1, source_target_pairs={{0,16},{16,0},{1,17},{17,1},{2,18},{18,2},{3,19},{19,3},{4,20},{20... | collective-permute-start | bytes 110600 | tf_op jit(solution)/shard_map/ppermute | solution.py:145
  154.3 0.0 collective-permute-done.5
  154.3 0.0 copy-done.3
  154.3 2.6 %fusion = f32[256,1152]{1,0:T(8,128)} fusion(bf16[512,256]{1,0:T(8,128)(2,1)S(1)} %bitcast.33, bf16[256,1152]{1,0:T(8,128)(2,1)} %collective-permute-done.5, bf16[256,1152]{1,0:T(8,128)(2,1)S(1)} %copy-done.3), kind=kOutput, calls=%fused_computation.1 | convolution fusion | flops 304349184 | bytes 2621440 | tf_op jit(solution)/shard_map/tf,td->fd/dot_general | solution.py:195
  156.9 4.4 %collective-permute-done.4 = bf16[16,1152]{1,0:T(8,128)(2,1)S(1)} collective-permute-done((bf16[16,1152]{1,0:T(8,128)(2,1)S(1)}, bf16[16,1152]{1,0:T(8,128)(2,1)S(1)}, u32[]{:S(2)}, u32[]{:S(2)}) %collective-permute-start.4) | collective-permute-done | bytes 36896 | tf_op jit(solution)/shard_map/ppermute | solution.py:145
  161.3 0.6 fusion.4
  161.9 1.8 %all-to-all-done.5 = bf16[16,2,36,512]{3,1,2,0:T(2,128)(2,1)S(1)} async-done(((bf16[16,2,36,512]{3,1,2,0:T(2,128)(2,1)}), bf16[16,2,36,512]{3,1,2,0:T(2,128)(2,1)S(1)}, u32[]{:S(2)}, u32[]{:S(2)}) %all-to-all-start.5) | async-done | bytes 1179680 | tf_op jit(solution)/shard_map/all_to_all | solution.py:137
  163.7 0.2 copy.21
  164.0 0.3 reshape.31
  164.3 1.5 fusion.10
  (9 shorter events, 0.2 us)
Async XLA Ops:
  0.6 18.7 %copy-start.7 = (bf16[512,36]{0,1:T(8,128)(2,1)S(1)}, bf16[512,36]{0,1:T(8,128)(2,1)}, u32[]{:S(2)}) copy-start(bf16[512,36]{0,1:T(8,128)(2,1)} %param.9) | copy-start | bytes 110596
  2.4 27.9 %all-to-all-start = ((bf16[16,2,2304]{2,1,0:T(2,128)(2,1)}), bf16[16,2,2304]{2,1,0:T(2,128)(2,1)S(1)}, u32[]{:S(2)}, u32[]{:S(2)}) async-start(bf16[16,2,2304]{2,1,0:T(2,128)(2,1)} %shard_map.94), calls=%async_computation | async-start | bytes 294912 | tf_op jit(solution)/shard_map/all_to_all | solution.py:137
  32.0 6.9 %copy-start.1 = (bf16[1152,256]{1,0:T(8,128)(2,1)S(1)}, bf16[1152,256]{1,0:T(8,128)(2,1)}, u32[]{:S(2)}) copy-start(bf16[1152,256]{1,0:T(8,128)(2,1)} %up_ref.2) | copy-start | bytes 1769476
  32.0 13.1 %copy-start = (bf16[256,1152]{1,0:T(8,128)(2,1)S(1)}, bf16[256,1152]{1,0:T(8,128)(2,1)}, u32[]{:S(2)}) copy-start(bf16[256,1152]{1,0:T(8,128)(2,1)} %down_ref) | copy-start | bytes 1769476
  32.0 34.4 %all-to-all-start.1 = ((bf16[16,32,2304]{2,1,0:T(8,128)(2,1)}), bf16[16,32,2304]{2,1,0:T(8,128)(2,1)S(1)}, u32[]{:S(2)}, u32[]{:S(2)}) async-start(bf16[16,32,2304]{2,1,0:T(8,128)(2,1)} %broadcast_in_dim.6), calls=%async_computation.1 | async-start | bytes 4718592 | tf_op jit(solution)/shard_map/all_to_all | solution.py:137
  38.9 23.4 %collective-permute-start = (bf16[1152,256]{1,0:T(8,128)(2,1)S(1)}, bf16[1152,256]{1,0:T(8,128)(2,1)}, u32[]{:S(2)}, u32[]{:S(2)}) collective-permute-start(bf16[1152,256]{1,0:T(8,128)(2,1)S(1)} %copy-done.1), channel_id=1, source_target_pairs={{0,1},{1,0},{2,3},{3,2},{4,5},{5,4},{6,7},{7,6},{8,9},{9,8},{10,11... | collective-permute-start | bytes 1769480 | tf_op jit(solution)/shard_map/ppermute | solution.py:145
  45.1 17.2 %collective-permute-start.1 = (bf16[256,1152]{1,0:T(8,128)(2,1)S(1)}, bf16[256,1152]{1,0:T(8,128)(2,1)}, u32[]{:S(2)}, u32[]{:S(2)}) collective-permute-start(bf16[256,1152]{1,0:T(8,128)(2,1)S(1)} %copy-done), channel_id=1, source_target_pairs={{0,1},{1,0},{2,3},{3,2},{4,5},{5,4},{6,7},{7,6},{8,9},{9,8},{10,11... | collective-permute-start | bytes 1769480 | tf_op jit(solution)/shard_map/ppermute | solution.py:145
  47.0 13.8 %collective-permute-start.2 = (bf16[36,512]{1,0:T(8,128)(2,1)}, bf16[36,512]{1,0:T(8,128)(2,1)}, u32[]{:S(2)}, u32[]{:S(2)}) collective-permute-start(bf16[36,512]{1,0:T(8,128)(2,1)} %fusion.5), channel_id=1, source_target_pairs={{0,16},{16,0},{1,17},{17,1},{2,18},{18,2},{3,19},{19,3},{4,20},{20... | collective-permute-start | bytes 110600 | tf_op jit(solution)/shard_map/ppermute | solution.py:145
  68.7 52.3 %copy-start.2 = (bf16[256,1152]{1,0:T(8,128)(2,1)}, bf16[256,1152]{1,0:T(8,128)(2,1)S(1)}, u32[]{:S(2)}) copy-start(bf16[256,1152]{1,0:T(8,128)(2,1)S(1)} %get-tuple-element.35) | copy-start | bytes 1769476
  68.7 52.3 %copy-start.4 = (bf16[256,1152]{1,0:T(8,128)(2,1)}, bf16[256,1152]{1,0:T(8,128)(2,1)S(1)}, u32[]{:S(2)}) copy-start(bf16[256,1152]{1,0:T(8,128)(2,1)S(1)} %get-tuple-element.36) | copy-start | bytes 1769476
  110.7 8.8 %collective-permute-start.3 = (bf16[8,2,32,256]{3,2,1,0:T(8,128)(2,1)S(1)}, bf16[8,2,32,256]{3,2,1,0:T(8,128)(2,1)S(1)}, u32[]{:S(2)}, u32[]{:S(2)}) collective-permute-start(bf16[8,2,32,256]{3,2,1,0:T(8,128)(2,1)S(1)} %all_to_all.31.own_ref), channel_id=1, source_target_pairs={{0,1},{1,0},{2,3},{3,2},{4,5},{5,4},{6,7},{7,6},{8,9},{9,8},{10,11... | collective-permute-start | bytes 786440 | tf_op jit(solution)/shard_map/ppermute | solution.py:145
  121.0 4.5 %copy-start.6 = (bf16[2,36,512]{2,1,0:T(8,128)(2,1)S(1)}, bf16[2,36,512]{2,1,0:T(8,128)(2,1)}, u32[]{:S(2)}) copy-start(bf16[2,36,512]{2,1,0:T(8,128)(2,1)} %maximum_select_fusion) | copy-start | bytes 221188
  121.0 21.6 %all-to-all-start.4 = ((bf16[16,32,1152]{2,1,0:T(8,128)(2,1)}), bf16[16,32,1152]{2,1,0:T(8,128)(2,1)S(1)}, u32[]{:S(2)}, u32[]{:S(2)}) async-start(bf16[16,32,1152]{2,1,0:T(8,128)(2,1)} %get-tuple-element.28), calls=%async_computation.4 | async-start | bytes 2359296 | tf_op jit(solution)/shard_map/all_to_all | solution.py:137
  125.6 1.7 %copy-start.5 = (bf16[256,1152]{1,0:T(8,128)(2,1)S(1)}, bf16[256,1152]{1,0:T(8,128)(2,1)}, u32[]{:S(2)}) copy-start(bf16[256,1152]{1,0:T(8,128)(2,1)} %copy-done.4) | copy-start | bytes 1769476
  127.3 27.0 %collective-permute-start.5 = (bf16[256,1152]{1,0:T(8,128)(2,1)S(1)}, bf16[256,1152]{1,0:T(8,128)(2,1)}, u32[]{:S(2)}, u32[]{:S(2)}) collective-permute-start(bf16[256,1152]{1,0:T(8,128)(2,1)S(1)} %copy-done.5), channel_id=1, source_target_pairs={{0,1},{1,0},{2,3},{3,2},{4,5},{5,4},{6,7},{7,6},{8,9},{9,8},{10,11... | collective-permute-start | bytes 1769480 | tf_op jit(solution)/shard_map/ppermute | solution.py:145
  142.8 21.0 %all-to-all-start.5 = ((bf16[16,2,36,512]{3,1,2,0:T(2,128)(2,1)}), bf16[16,2,36,512]{3,1,2,0:T(2,128)(2,1)S(1)}, u32[]{:S(2)}, u32[]{:S(2)}) async-start(bf16[16,2,36,512]{3,1,2,0:T(2,128)(2,1)} %broadcast_in_dim.8), calls=%async_computation.5 | async-start | bytes 2359296 | tf_op jit(solution)/shard_map/all_to_all | solution.py:137
  147.5 6.8 %copy-start.3 = (bf16[256,1152]{1,0:T(8,128)(2,1)S(1)}, bf16[256,1152]{1,0:T(8,128)(2,1)}, u32[]{:S(2)}) copy-start(bf16[256,1152]{1,0:T(8,128)(2,1)} %copy-done.2) | copy-start | bytes 1769476
  147.7 13.6 %collective-permute-start.4 = (bf16[16,1152]{1,0:T(8,128)(2,1)S(1)}, bf16[16,1152]{1,0:T(8,128)(2,1)S(1)}, u32[]{:S(2)}, u32[]{:S(2)}) collective-permute-start(bf16[16,1152]{1,0:T(8,128)(2,1)S(1)} %fusion.6), channel_id=1, source_target_pairs={{0,16},{16,0},{1,17},{17,1},{2,18},{18,2},{3,19},{19,3},{4,20},{20... | collective-permute-start | bytes 110600 | tf_op jit(solution)/shard_map/ppermute | solution.py:145
